TPU v7x, 128 devices: a whole 4x4x4 slice. The times are simulated.
128 devices in a mesh: row: 8 (over y, z_lo), col: 16 (over x, z_hi, core).
Axes of the slice: x: 4, y: 4, z: 4 (z_hi: 2, z_lo: 2; z = z_hi * 2 + z_lo), core: 2. Of those that a mesh axis runs over, the one named last changes fastest.
Arguments:
- tokens: bfloat16 [2048, 8192], P('col', 'row'), may hold values from -6 to 6
- w1_blocks: bfloat16 [8, 16, 8, 256, 256], P('row', 'col'), may hold values from -0.1875 to 0.1875
- w2_blocks: bfloat16 [16, 8, 8, 256, 256], P('col', 'row'), may hold values from -0.09375 to 0.09375
- block_places: int32 [8, 16, 8], P('row', 'col'), may hold values from 0 to 31, as said below
- counts: int32 [8, 16], P('row', 'col'), may hold values from 1 to 8
- cotangent: bfloat16 [2048, 8192], P('col', 'row'), may hold values from -6 to 6
Outputs:
- output: bfloat16 [2048, 8192], P('col', 'row')
- input_grad: bfloat16 [2048, 8192], P('col', 'row')
- first_grad: bfloat16 [8, 16, 8, 256, 256], P('row', 'col')
- second_grad: bfloat16 [16, 8, 8, 256, 256], P('col', 'row')
Inputs may be any that keep to these rules, and one draw needn't show every extreme that they name: `block_places`: within each tile the 8 positions are distinct; position p stands for the tile's model-width block p // 8 and hidden block p % 8; only the first counts of them are live.
All inputs are finite; a program needn't handle non-finite values.
Results may differ from a plain program's by a relative error of at most 0.025.
Values may be sent and summed in bfloat16 or wider, within the bound.
A program may use at most 128 MiB of HBM per device.

v0:
```python
import math

import jax
import jax.numpy as jnp
from jax import lax
from jax.sharding import PartitionSpec as P

F = 32768
BLK = 256


gelu_scale = math.sqrt(2.0 / math.pi)
gelu_cubic = 0.044715


def gelu_pair(hidden):
    inner = gelu_scale * (hidden + gelu_cubic * hidden * hidden * hidden)
    tanh_value = jnp.tanh(inner)
    value = 0.5 * hidden * (1.0 + tanh_value)
    slope = 0.5 * (1.0 + tanh_value) + 0.5 * hidden * (
        1.0 - tanh_value * tanh_value
    ) * gelu_scale * (1.0 + 3.0 * gelu_cubic * hidden * hidden)
    return (value, slope)


def local_sum(source, weights, from_blocks, to_blocks, count, width, flipped):

    def local_advance(slot, total):
        columns = lax.dynamic_slice_in_dim(source, from_blocks[slot] * BLK, BLK, 1)
        if flipped:
            product = lax.dot_general(
                columns, weights[slot], (((1,), (1,)), ((), ())), preferred_element_type=jnp.float32
            )
        else:
            product = jnp.dot(columns, weights[slot], preferred_element_type=jnp.float32)
        current = lax.dynamic_slice_in_dim(total, to_blocks[slot] * BLK, BLK, 1)
        return lax.dynamic_update_slice_in_dim(total, current + product, to_blocks[slot] * BLK, 1)

    start = jnp.zeros((source.shape[0], width), jnp.float32)
    return lax.fori_loop(0, count, local_advance, start)


def slot_grads(left, right, left_blocks, right_blocks, count):

    def slot_advance(slot, grads):
        left_cols = lax.dynamic_slice_in_dim(left, left_blocks[slot] * BLK, BLK, 1)
        right_cols = lax.dynamic_slice_in_dim(right, right_blocks[slot] * BLK, BLK, 1)
        product = lax.dot_general(
            left_cols, right_cols, (((0,), (0,)), ((), ())), preferred_element_type=jnp.float32
        )
        return lax.dynamic_update_index_in_dim(grads, product.astype(jnp.bfloat16), slot, 0)

    start = jnp.zeros((left_blocks.shape[0], BLK, BLK), jnp.bfloat16)
    return lax.fori_loop(0, count, slot_advance, start)


def per_device(tokens, w1_blocks, w2_blocks, block_places, counts, cotangent):
    model_local = tokens.shape[1]
    hidden_local = F // lax.axis_size("col")
    hidden_blocks = hidden_local // BLK
    places = block_places[0, 0]
    count = counts[0, 0]
    width_block = places // hidden_blocks
    hidden_block = places % hidden_blocks
    first = w1_blocks[0, 0]
    second = w2_blocks[0, 0]
    inputs_all = lax.all_gather(tokens, "col", axis=0, tiled=True)
    hidden_part = local_sum(
        inputs_all, first, width_block, hidden_block, count, hidden_local, False
    )
    hidden_rows = lax.psum_scatter(
        hidden_part.astype(jnp.bfloat16), "row", scatter_dimension=0, tiled=True
    ).astype(jnp.float32)
    gelu_value, gelu_slope = gelu_pair(hidden_rows)
    activated = lax.all_gather(gelu_value.astype(jnp.bfloat16), "row", axis=0, tiled=True)
    output_part = local_sum(activated, second, hidden_block, width_block, count, model_local, False)
    output = lax.psum_scatter(
        output_part.astype(jnp.bfloat16), "col", scatter_dimension=0, tiled=True
    )
    cotangent_all = lax.all_gather(cotangent, "col", axis=0, tiled=True)
    grad_part = local_sum(
        cotangent_all, second, width_block, hidden_block, count, hidden_local, True
    )
    grad_rows = lax.psum_scatter(
        grad_part.astype(jnp.bfloat16), "row", scatter_dimension=0, tiled=True
    ).astype(jnp.float32)
    hidden_grad = lax.all_gather(
        (grad_rows * gelu_slope).astype(jnp.bfloat16), "row", axis=0, tiled=True
    )
    input_part = local_sum(hidden_grad, first, hidden_block, width_block, count, model_local, True)
    input_grad = lax.psum_scatter(
        input_part.astype(jnp.bfloat16), "col", scatter_dimension=0, tiled=True
    )
    first_grad = slot_grads(inputs_all, hidden_grad, width_block, hidden_block, count)
    second_grad = slot_grads(activated, cotangent_all, hidden_block, width_block, count)
    return (output, input_grad, first_grad[None, None], second_grad[None, None])


def solution(mesh):
    return jax.shard_map(
        per_device,
        mesh=mesh,
        in_specs=(
            P("col", "row"),
            P("row", "col", None, None, None),
            P("col", "row", None, None, None),
            P("row", "col", None),
            P("row", "col"),
            P("col", "row"),
        ),
        out_specs=(
            P("col", "row"),
            P("col", "row"),
            P("row", "col", None, None, None),
            P("col", "row", None, None, None),
        ),
        check_vma=False,
    )
```

profile of v0, /device:TPU:0, one launch (start us, length us, event | category | flops | bytes accessed | tf_op | source)
XLA Modules:
  0.0 1013.2 jit_solution(2648447219703666945)
XLA Ops:
  9.4 59.6 %all-gather.5.cloned.1.call-done = bf16[2048,1024]{1,0:T(8,128)(2,1)} async-done(((bf16[128,1024]{1,0:T(8,128)(2,1)}), bf16[2048,1024]{1,0:T(8,128)(2,1)}) %all-gather.5.cloned.1.call-update) | async-done | bytes 4194320 | tf_op jit(solution)/shard_map/all_gather | solution.py:67
  68.9 7.9 broadcast.35.clone
  76.8 21.7 %while.60 = (s32[]{:T(128)}, f32[2048,2048]{1,0:T(8,128)}, s32[]{:T(128)}, s32[8]{0:T(128)S(1)}, s32[8]{0:T(128)S(1)}, /*index=5*/bf16[2048,1024]{1,0:T(8,128)(2...) while((s32[]{:T(128)}, f32[2048,2048]{1,0:T(8,128)}, ...), condition=%wide.region_1.2_spmd, body=%wide.region_0.1_spmd.sunk | while | flops 268959744 | bytes 5374239 | solution.py:40
  98.5 9.2 convert_element_type.30
  107.9 18.2 %all-gather.9.cloned.1.call-done = bf16[2048,1024]{1,0:T(8,128)(2,1)} async-done(((bf16[128,1024]{1,0:T(8,128)(2,1)}), bf16[2048,1024]{1,0:T(8,128)(2,1)}) %all-gather.9.cloned.1.call-update) | async-done | bytes 4194320 | tf_op jit(solution)/shard_map/all_gather | solution.py:80
  126.1 7.9 broadcast.35.clone.1
  133.9 21.7 %while.62 = (s32[]{:T(128)}, f32[2048,2048]{1,0:T(8,128)}, s32[]{:T(128)}, s32[8]{0:T(128)S(1)}, s32[8]{0:T(128)S(1)}, /*index=5*/bf16[2048,1024]{1,0:T(8,128)(2...) while((s32[]{:T(128)}, f32[2048,2048]{1,0:T(8,128)}, ...), condition=%wide.region_7.8_spmd, body=%wide.region_6.7_spmd.sunk | while | flops 268959744 | bytes 5374239 | solution.py:40
  155.7 9.0 convert_element_type.34
  164.8 144.7 %reduce-scatter.5.cloned.1.call-done = bf16[256,2048]{1,0:T(8,128)(2,1)} async-done(((bf16[2048,2048]{1,0:T(8,128)(2,1)}), bf16[256,2048]{1,0:T(8,128)(2,1)}) %reduce-scatter.5.cloned.1.call-update) | async-done | bytes 1048592 | tf_op jit(solution)/shard_map/reduce_scatter | solution.py:71
  309.5 172.5 %reduce-scatter.9.cloned.1.call-done = bf16[256,2048]{1,0:T(8,128)(2,1)} async-done(((bf16[2048,2048]{1,0:T(8,128)(2,1)}), bf16[256,2048]{1,0:T(8,128)(2,1)}) %reduce-scatter.9.cloned.1.call-update) | async-done | bytes 1048592 | tf_op jit(solution)/shard_map/reduce_scatter | solution.py:84
  481.9 4.4 fusion.37
  487.0 168.9 %all-gather.11.cloned.1.call-done = bf16[2048,2048]{1,0:T(8,128)(2,1)} async-done(((bf16[256,2048]{1,0:T(8,128)(2,1)}), bf16[2048,2048]{1,0:T(8,128)(2,1)}) %all-gather.11.cloned.1.call-update) | async-done | bytes 8388624 | tf_op jit(solution)/shard_map/all_gather | solution.py:87
  655.9 4.3 broadcast.33.clone.1
  660.2 21.8 %while.63 = (s32[]{:T(128)}, f32[2048,1024]{1,0:T(8,128)}, s32[]{:T(128)}, s32[8]{0:T(128)S(1)}, s32[8]{0:T(128)S(1)}, /*index=5*/bf16[2048,2048]{1,0:T(8,128)(2...) while((s32[]{:T(128)}, f32[2048,1024]{1,0:T(8,128)}, ...), condition=%wide.region_10.11_spmd, body=%wide.region_9.10_spmd.sunk | while | flops 268959744 | bytes 5374239 | solution.py:40
  682.0 6.0 convert_element_type.37
  688.1 143.7 %all-gather.7.cloned.1.call-done = bf16[2048,2048]{1,0:T(8,128)(2,1)} async-done(((bf16[256,2048]{1,0:T(8,128)(2,1)}), bf16[2048,2048]{1,0:T(8,128)(2,1)}) %all-gather.7.cloned.1.call-update) | async-done | bytes 8388624 | tf_op jit(solution)/shard_map/all_gather | solution.py:75
  831.7 4.3 broadcast.33.clone
  836.0 21.8 %while.61 = (s32[]{:T(128)}, f32[2048,1024]{1,0:T(8,128)}, s32[]{:T(128)}, s32[8]{0:T(128)S(1)}, s32[8]{0:T(128)S(1)}, /*index=5*/bf16[2048,2048]{1,0:T(8,128)(2...) while((s32[]{:T(128)}, f32[2048,1024]{1,0:T(8,128)}, ...), condition=%wide.region_4.5_spmd, body=%wide.region_3.4_spmd.sunk | while | flops 268959744 | bytes 5374239 | solution.py:40
  853.1 4.0 fusion.64
  857.8 6.4 convert_element_type.33
  864.3 16.3 %while.64 = (s32[]{:T(128)}, bf16[8,256,256]{2,1,0:T(8,128)(2,1)S(1)}, s32[]{:T(128)}, s32[8]{0:T(128)S(1)}, bf16[2048,1024]{1,0:T(8,128)(2,1)}, /*index=5*/s32[...) while((s32[]{:T(128)}, ...), condition=%wide.region_13.14_spmd, body=%wide.region_12.13_spmd.sunk | while | flops 268500992 | bytes 2228511 | solution.py:54
  881.6 16.3 %while.65 = (s32[]{:T(128)}, bf16[8,256,256]{2,1,0:T(8,128)(2,1)S(1)}, s32[]{:T(128)}, s32[8]{0:T(128)S(1)}, bf16[2048,2048]{1,0:T(8,128)(2,1)}, /*index=5*/s32[...) while((s32[]{:T(128)}, ...), condition=%wide.region_15.16_spmd, body=%wide.region_14.15_spmd.sunk | while | flops 268500992 | bytes 2228511 | solution.py:54
  897.9 24.4 %reduce-scatter.11.cloned.1.call-done = bf16[128,1024]{1,0:T(8,128)(2,1)} async-done(((bf16[2048,1024]{1,0:T(8,128)(2,1)}), bf16[128,1024]{1,0:T(8,128)(2,1)}) %reduce-scatter.11.cloned.1.call-update) | async-done | bytes 262160 | tf_op jit(solution)/shard_map/reduce_scatter | solution.py:91
  922.3 84.1 %reduce-scatter.7.cloned.1.call-done = bf16[128,1024]{1,0:T(8,128)(2,1)} async-done(((bf16[2048,1024]{1,0:T(8,128)(2,1)}), bf16[128,1024]{1,0:T(8,128)(2,1)}) %reduce-scatter.7.cloned.1.call-update) | async-done | bytes 262160 | tf_op jit(solution)/shard_map/reduce_scatter | solution.py:77
  (76 shorter events, 79.9 us)
Async XLA Ops:
  7.2 61.8 %all-gather.5.cloned.1.call-start = ((), (), s32[]{:S(2)}) async-start(), calls=%async_computation.4 | async-start | bytes 4456448 | tf_op jit(solution)/shard_map/all_gather | solution.py:67
  7.9 118.2 %all-gather.9.cloned.1.call-start = ((), (), s32[]{:S(2)}) async-start(), calls=%async_computation.8 | async-start | bytes 4456448 | tf_op jit(solution)/shard_map/all_gather | solution.py:80
  8.6 300.8 %reduce-scatter.5.cloned.1.call-start = ((), (), s32[]{:S(2)}) async-start(), calls=%async_computation.5 | async-start | bytes 9437184 | tf_op jit(solution)/shard_map/reduce_scatter | solution.py:71
  107.8 374.1 %reduce-scatter.9.cloned.1.call-start = ((), (), s32[]{:S(2)}) async-start(), calls=%async_computation.9 | async-start | bytes 9437184 | tf_op jit(solution)/shard_map/reduce_scatter | solution.py:84
  164.7 491.1 %all-gather.11.cloned.1.call-start = ((), (), s32[]{:S(2)}) async-start(), calls=%async_computation.10 | async-start | bytes 9437184 | tf_op jit(solution)/shard_map/all_gather | solution.py:87
  486.4 345.3 %all-gather.7.cloned.1.call-start = ((), (), s32[]{:S(2)}) async-start(), calls=%async_computation.6 | async-start | bytes 9437184 | tf_op jit(solution)/shard_map/all_gather | solution.py:75
  487.0 435.3 %reduce-scatter.11.cloned.1.call-start = ((), (), s32[]{:S(2)}) async-start(), calls=%async_computation.11 | async-start | bytes 4456448 | tf_op jit(solution)/shard_map/reduce_scatter | solution.py:91
  688.0 318.4 %reduce-scatter.7.cloned.1.call-start = ((), (), s32[]{:S(2)}) async-start(), calls=%async_computation.7 | async-start | bytes 4456448 | tf_op jit(solution)/shard_map/reduce_scatter | solution.py:77
  880.6 1.0 copy-start.1
  897.9 108.5 %copy-start = (bf16[8,256,256]{2,1,0:T(8,128)(2,1)}, bf16[8,256,256]{2,1,0:T(8,128)(2,1)S(1)}, u32[]{:S(2)}) copy-start(bf16[8,256,256]{2,1,0:T(8,128)(2,1)S(1)} %get-tuple-element.237) | copy-start | bytes 3145732
Sparse Core Ops, SparseCore 0:
  10.4 58.4 all-gather.4
  71.3 54.7 all-gather.8
  128.5 180.9 reduce-scatter.4
  311.7 170.1 reduce-scatter.8
  486.5 169.3 all-gather.10
  657.9 173.7 all-gather.6
  836.3 85.8 reduce-scatter.10
  927.4 78.8 reduce-scatter.6
where the time goes:
time: 1020 us; the launch traced here: 1010 us
  waiting for transfers between devices  818 us (80%)
  matrix products  58.8 us (6%)
  local copies, waits for them, and re-layouts  46.5 us (5%)
  loops' own time  39.6 us (4%)
  other arithmetic  35.8 us (4%)
  between operations  14.2 us (1%)
    reduce_scatter x1, waiting for transfers between devices, per_device(): lax.psum_scatter(grad_part.astype(jnp.bfloat16), 'row', scatter_dimension...  172 us
    all_gather x1, waiting for transfers between devices, per_device(): lax.all_gather((grad_rows * gelu_slope).astype(jnp.bfloat16), 'row', axis...  169 us
    reduce_scatter x1, waiting for transfers between devices, per_device(): lax.psum_scatter(hidden_part.astype(jnp.bfloat16), 'row', scatter_dimensi...  145 us
    all_gather x1, waiting for transfers between devices, per_device(): lax.all_gather(gelu_value.astype(jnp.bfloat16), 'row', axis=0, tiled=True)  144 us
    reduce_scatter x1, waiting for transfers between devices, per_device(): lax.psum_scatter(output_part.astype(jnp.bfloat16), 'col', scatter_dimensi...  84.1 us
    all_gather x1, waiting for transfers between devices, per_device(): inputs_all = lax.all_gather(tokens, 'col', axis=0, tiled=True)  59.6 us
    another operation x4, loops' own time, local_sum(): return lax.fori_loop(0, count, local_advance, start)  26.4 us
    another operation x6, local copies, waits for them, and re-layouts  24.5 us
  transfers between devices with their start and end apart: 8, of which 8 were waited for; matrix products, arithmetic and copies ran while one was open for 13% of the time, Pallas kernels for 0%

commit v1 on v0

v1 whole, which is shorter than its diff:
```python
import functools
import math

import jax
import jax.numpy as jnp
from jax import lax
from jax.experimental import pallas as pl
from jax.experimental.pallas import tpu as pltpu
from jax.sharding import PartitionSpec as P

BLK = 256
SLOTS = 8
HIDDEN_BLOCKS = 8
QUARTER = 32
WIDTH = 1024
ROWS = 512
bf16 = jnp.bfloat16
f32 = jnp.float32

gelu_scale = math.sqrt(2.0 / math.pi)
gelu_cubic = 0.044715
MIB = 1 << 20


def gelu_pair(hidden):
    inner = gelu_scale * (hidden + gelu_cubic * hidden * hidden * hidden)
    tanh_value = jnp.tanh(inner)
    value = 0.5 * hidden * (1.0 + tanh_value)
    slope = 0.5 * (1.0 + tanh_value) + 0.5 * hidden * (
        1.0 - tanh_value * tanh_value
    ) * gelu_scale * (1.0 + 3.0 * gelu_cubic * hidden * hidden)
    return (value, slope)


def y_index():
    return lax.div(lax.axis_index("row"), 2)


def peer(dx=0, dy=0, zl=0, zh=0, core=0):
    k, j = lax.axis_index("row"), lax.axis_index("col")
    row = lax.rem(lax.div(k, 2) + dy, 4) * 2 + lax.rem(lax.rem(k, 2) + zl, 2)
    col = (
        lax.rem(lax.div(j, 4) + dx, 4) * 4
        + lax.rem(lax.rem(lax.div(j, 2), 2) + zh, 2) * 2
        + lax.rem(lax.rem(j, 2) + core, 2)
    )
    return (row, col)


Y_PEERS = [dict(dy=1), dict(dy=2), dict(dy=3)]
X_PEERS = [dict(dx=1), dict(dx=3)]
CORE_PEER, ZH_PEER, ZL_PEER = dict(core=1), dict(zh=1), dict(zl=1)


def greet(peers):
    barrier = pltpu.get_barrier_semaphore()
    for one in peers:
        pl.semaphore_signal(barrier, inc=1, device_id=peer(**one), device_id_type=pl.DeviceIdType.MESH)
    pl.semaphore_wait(barrier, len(peers))


class Copies:
    def __init__(self, send, recv):
        self.send, self.recv, self.made = send, recv, []

    def start(self, src, dst, **to):
        n = len(self.made)
        copy = pltpu.make_async_remote_copy(
            src_ref=src, dst_ref=dst, send_sem=self.send.at[n], recv_sem=self.recv.at[n],
            device_id=peer(**to), device_id_type=pl.DeviceIdType.MESH,
        )
        copy.start()
        self.made.append(copy)
        return copy

    def finish(self):
        for copy in self.made:
            copy.wait_send()


def ring_gather_start(copies, own, dest, axis):
    up, down = {axis: 1}, {axis: 3}
    half = own.shape[0] // 2
    lo, hi = pl.ds(0, half), pl.ds(half, half)
    up_lo = copies.start(own.at[lo], dest.at[3, lo], **up)
    down_hi = copies.start(own.at[hi], dest.at[1, hi], **down)
    up_hi = copies.start(own.at[hi], dest.at[3, hi], **up)
    down_lo = copies.start(own.at[lo], dest.at[1, lo], **down)
    return (up_lo, down_hi, up_hi, down_lo)


def ring_gather_forward(copies, begun, dest, axis):
    up, down = {axis: 1}, {axis: 3}
    half = dest.shape[1] // 2
    lo, hi = pl.ds(0, half), pl.ds(half, half)
    begun[0].wait_recv()
    on_up = copies.start(dest.at[3, lo], dest.at[2, lo], **up)
    begun[1].wait_recv()
    on_down = copies.start(dest.at[1, hi], dest.at[2, hi], **down)
    return (begun[2], begun[3], on_up, on_down)


def rows_of(core, x, zh):
    return ((core * 4 + x) * 2 + zh) * QUARTER


def gather_kernel(tok, cot, w1, tab, tok_all, cot_all, w1_all, tab_all, send, recv, local):
    greet(Y_PEERS + X_PEERS + [CORE_PEER, ZH_PEER])
    copies = Copies(send, recv)
    y = y_index()
    pairs = ((tok, tok_all), (cot, cot_all))
    half = pl.ds(0, QUARTER)
    locals_ = []
    for n, (src, dst) in enumerate(pairs):
        rows = pl.ds(pl.multiple_of(y * QUARTER, QUARTER), QUARTER)
        locals_.append(pltpu.make_async_copy(src.at[rows], dst.at[0, half], local.at[n]))
    locals_.append(pltpu.make_async_copy(w1, w1_all.at[0], local.at[2]))
    locals_.append(pltpu.make_async_copy(tab, tab_all.at[0], local.at[3]))
    for copy in locals_:
        copy.start()
    spread = []
    for src, dst in pairs:
        here = []
        for r in (1, 3, 2):
            rows = pl.ds(pl.multiple_of(lax.rem(y + r, 4) * QUARTER, QUARTER), QUARTER)
            here.append(copies.start(src.at[rows], dst.at[4 - r, half], dy=r))
        spread.append(here)
    tabs = [copies.start(tab, tab_all.at[4 - r], dy=r) for r in (1, 2, 3)]
    w_begun = ring_gather_start(copies, w1, w1_all, "dy")

    def part(core, x, zh, count=1):
        return (slice(None), pl.ds(rows_of(core, x, zh), count * QUARTER))

    across, first = [], []
    for n, (src, dst) in enumerate(pairs):
        locals_[n].wait()
        for copy in spread[n]:
            copy.wait_recv()
        own = dst.at[part(0, 0, 0)]
        across.append(copies.start(own, dst.at[part(0, 0, 1)], zh=1))
        first.append((
            copies.start(own, dst.at[part(0, 3, 0)], dx=1),
            copies.start(own, dst.at[part(0, 1, 0)], dx=3),
        ))
    second, over = [], []
    for n, (src, dst) in enumerate(pairs):
        across[n].wait_recv()
        own = dst.at[part(0, 0, 1)]
        second.append((
            copies.start(own, dst.at[part(0, 3, 1)], dx=1),
            copies.start(own, dst.at[part(0, 1, 1)], dx=3),
        ))
        over.append(copies.start(dst.at[part(0, 0, 0, 2)], dst.at[part(1, 0, 0, 2)], core=1))
    w_rest = ring_gather_forward(copies, w_begun, w1_all, "dy")
    onward = []
    for n, (src, dst) in enumerate(pairs):
        first[n][0].wait_recv()
        on_up = copies.start(dst.at[part(0, 3, 0)], dst.at[part(0, 2, 0)], dx=1)
        second[n][1].wait_recv()
        on_down = copies.start(dst.at[part(0, 1, 1)], dst.at[part(0, 2, 1)], dx=3)
        onward.append((on_up, on_down))
    for n, (src, dst) in enumerate(pairs):
        second[n][0].wait_recv()
        over.append(copies.start(dst.at[part(0, 3, 0, 2)], dst.at[part(1, 3, 0, 2)], core=1))
        first[n][1].wait_recv()
        over.append(copies.start(dst.at[part(0, 1, 0, 2)], dst.at[part(1, 1, 0, 2)], core=1))
    for n, (src, dst) in enumerate(pairs):
        for copy in onward[n]:
            copy.wait_recv()
        over.append(copies.start(dst.at[part(0, 2, 0, 2)], dst.at[part(1, 2, 0, 2)], core=1))
    for copy in tabs + over + list(w_rest):
        copy.wait_recv()
    locals_[2].wait()
    locals_[3].wait()
    copies.finish()


def exchange_start(copies, own, other):
    step = own.shape[0] // 4
    return [
        copies.start(own.at[pl.ds(n * step, step)], other.at[pl.ds(n * step, step)], zl=1)
        for n in range(4)
    ]


def second_kernel(w2, part, w2_all, other, send, recv, local):
    greet([dict(dy=1), dict(dy=3), ZL_PEER])
    copies = Copies(send, recv)
    mine = pltpu.make_async_copy(w2, w2_all.at[0], local.at[0])
    mine.start()
    begun = ring_gather_start(copies, w2, w2_all, "dy")
    swap = exchange_start(copies, part, other)
    rest = ring_gather_forward(copies, begun, w2_all, "dy")
    for copy in list(rest) + swap:
        copy.wait_recv()
    mine.wait()
    copies.finish()


def add_into(dst, *terms):
    def step(n, carry):
        total = terms[0][n].astype(f32)
        for term in terms[1:]:
            total = total + term[n].astype(f32)
        dst[n] = total.astype(dst.dtype)
        return carry

    lax.fori_loop(0, dst.shape[0], step, 0)


class RingReduce:
    def __init__(self, copies, part, far, near, axis):
        self.copies, self.part, self.far, self.near = copies, part, far, near
        self.up, self.down = {axis: 1}, {axis: 3}

    def start_far(self):
        self.far_up = self.copies.start(self.part(2, 0), self.far.at[0], **self.up)
        self.far_down = self.copies.start(self.part(2, 1), self.far.at[1], **self.down)

    def start_near(self):
        self.near_up = self.copies.start(self.part(1, 1), self.near.at[0, 1], **self.up)
        self.near_down = self.copies.start(self.part(3, 0), self.near.at[1, 0], **self.down)

    def onward(self):
        self.far_up.wait_recv()
        add_into(self.far.at[0], self.far.at[0], self.part(1, 0))
        self.last_up = self.copies.start(self.far.at[0], self.near.at[0, 0], **self.up)
        self.far_down.wait_recv()
        add_into(self.far.at[1], self.far.at[1], self.part(3, 1))
        self.last_down = self.copies.start(self.far.at[1], self.near.at[1, 1], **self.down)

    def finish(self, dst):
        for copy in (self.near_up, self.near_down, self.last_up, self.last_down):
            copy.wait_recv()
        for h in range(2):
            add_into(dst(h), self.part(0, h), self.near.at[0, h], self.near.at[1, h])


def weight_part(partial):
    return lambda r, h: partial.at[r, pl.ds(h * 4, 4)]


class OutputReduce:
    def __init__(self, copies, partial, arrived, far, near):
        self.copies, self.partial, self.arrived = copies, partial, arrived
        self.ring = RingReduce(
            copies, lambda r, h: arrived.at[:, pl.ds(r * 64 + h * 32, 32)], far, near, "dx")

    def start(self):
        self.over = {}
        for r in (2, 1, 3, 0):
            self.over[r] = self.copies.start(
                self.partial.at[:, pl.ds(256 + 64 * r, 64)], self.arrived.at[:, pl.ds(64 * r, 64)], core=1)

    def join(self, r):
        self.over[r].wait_recv()
        rows = pl.ds(64 * r, 64)
        add_into(self.arrived.at[:, rows], self.arrived.at[:, rows], self.partial.at[:, rows])

    def begin_ring(self):
        self.join(2)
        self.ring.start_far()
        self.join(1)
        self.join(3)
        self.ring.start_near()
        self.join(0)


def reduce_kernel(grad_part, second_part, out_part, grad_other, second_grad, out_mid,
                  far_w, near_w, arrived, far_x, near_x, send, recv):
    greet([dict(dy=1), dict(dy=3), ZL_PEER, CORE_PEER] + X_PEERS)
    copies = Copies(send, recv)
    weights = RingReduce(copies, weight_part(second_part), far_w, near_w, "dy")
    weights.start_far()
    swap = exchange_start(copies, grad_part, grad_other)
    out = OutputReduce(copies, out_part, arrived, far_x, near_x)
    out.start()
    weights.start_near()
    out.begin_ring()
    weights.onward()
    out.ring.onward()
    out.ring.finish(lambda h: out_mid.at[:, pl.ds(32 * h, 32)])
    weights.finish(lambda h: second_grad.at[pl.ds(4 * h, 4)])
    for copy in swap:
        copy.wait_recv()
    copies.finish()


class Home:
    def __init__(self, copies, mid, arrived, output, local):
        self.copies, self.mid, self.arrived, self.output, self.local = copies, mid, arrived, output, local

    def start(self):
        self.over = self.copies.start(self.mid.at[:, pl.ds(32, 32)], self.arrived, zh=1)

    def send(self):
        self.over.wait_recv()
        add_into(self.arrived, self.arrived, self.mid.at[:, pl.ds(0, 32)])
        rows = pl.ds(pl.multiple_of(y_index() * QUARTER, QUARTER), QUARTER)
        self.mine = pltpu.make_async_copy(self.arrived.at[0], self.output.at[rows], self.local)
        self.mine.start()
        self.sent = [self.copies.start(self.arrived.at[r], self.output.at[rows], dy=r) for r in (2, 1, 3)]

    def finish(self):
        self.mine.wait()
        for copy in self.sent:
            copy.wait_recv()


def last_kernel(first_part, in_part, out_mid, first_grad, output, input_grad,
                far_w, near_w, arrived, far_x, near_x, in_mid, home_out, home_in, send, recv, local):
    greet(Y_PEERS + X_PEERS + [CORE_PEER, ZH_PEER])
    copies = Copies(send, recv)
    weights = RingReduce(copies, weight_part(first_part), far_w, near_w, "dy")
    weights.start_far()
    into = OutputReduce(copies, in_part, arrived, far_x, near_x)
    into.start()
    out_home = Home(copies, out_mid, home_out, output, local.at[0])
    out_home.start()
    weights.start_near()
    into.begin_ring()
    out_home.send()
    weights.onward()
    into.ring.onward()
    into.ring.finish(lambda h: in_mid.at[:, pl.ds(32 * h, 32)])
    in_home = Home(copies, in_mid, home_in, input_grad, local.at[1])
    in_home.start()
    in_home.send()
    weights.finish(lambda h: first_grad.at[pl.ds(4 * h, 4)])
    out_home.finish()
    in_home.finish()
    copies.finish()


def columns(d):
    return pl.ds(pl.multiple_of(d * BLK, BLK), BLK)


def dot(a, b, da, db):
    return lax.dot_general(a, b, (((da,), (db,)), ((), ())), preferred_element_type=f32)


def hidden_kernel(tab, tok, w1, out, total):
    t = pl.program_id(0)

    @pl.when(t == 0)
    def _():
        total[...] = jnp.zeros_like(total)

    def step(s, carry):
        place = tab[t, 0, s]
        d, h = lax.div(place, HIDDEN_BLOCKS), lax.rem(place, HIDDEN_BLOCKS)
        total[h] += dot(tok[0, :, columns(d)], w1[0, s], 1, 0)
        return carry

    lax.fori_loop(0, tab[t, 0, SLOTS], step, 0)

    @pl.when(t == 3)
    def _():
        out[...] = total[...].astype(bf16)


CHUNK = 64


def forward_kernel(tab, mine, other, cot, w2, grad_part, out_part, second_part, slope, act, grad, out):
    t = pl.program_id(0)

    @pl.when(t == 0)
    def _():
        grad[...] = jnp.zeros_like(grad)

        def activate(n, carry):
            h, rows = lax.div(n, ROWS // CHUNK), pl.ds(pl.multiple_of(lax.rem(n, ROWS // CHUNK) * CHUNK, CHUNK), CHUNK)
            value, derivative = gelu_pair(mine[h, rows].astype(f32) + other[h, rows].astype(f32))
            act[h, rows] = value.astype(bf16)
            slope[h, rows] = derivative
            return carry

        lax.fori_loop(0, HIDDEN_BLOCKS * (ROWS // CHUNK), activate, 0)

    out[...] = jnp.zeros_like(out)

    def step(s, carry):
        place = tab[t, 0, s]
        d, h = lax.div(place, HIDDEN_BLOCKS), lax.rem(place, HIDDEN_BLOCKS)
        live = act[h]
        back = cot[0, :, columns(d)]
        weight = w2[0, s]
        grad[h] += dot(back, weight, 1, 1)
        out[:, columns(d)] += dot(live, weight, 1, 0)
        second_part[0, s] = dot(live, back, 0, 0).astype(bf16)
        return carry

    def dead(s, carry):
        second_part[0, s] = jnp.zeros((BLK, BLK), bf16)
        return carry

    count = tab[t, 0, SLOTS]
    lax.fori_loop(0, count, step, 0)
    lax.fori_loop(count, SLOTS, dead, 0)
    out_part[0] = out[...].astype(bf16)

    @pl.when(t == 3)
    def _():
        grad_part[...] = grad[...].astype(bf16)


def backward_kernel(tab, mine, other, slope, tok, w1, in_part, first_part, grad, out):
    t = pl.program_id(0)

    @pl.when(t == 0)
    def _():

        def combine(n, carry):
            h, rows = lax.div(n, ROWS // CHUNK), pl.ds(pl.multiple_of(lax.rem(n, ROWS // CHUNK) * CHUNK, CHUNK), CHUNK)
            total = mine[h, rows].astype(f32) + other[h, rows].astype(f32)
            grad[h, rows] = (total * slope[h, rows]).astype(bf16)
            return carry

        lax.fori_loop(0, HIDDEN_BLOCKS * (ROWS // CHUNK), combine, 0)

    out[...] = jnp.zeros_like(out)

    def step(s, carry):
        place = tab[t, 0, s]
        d, h = lax.div(place, HIDDEN_BLOCKS), lax.rem(place, HIDDEN_BLOCKS)
        back = grad[h]
        out[:, columns(d)] += dot(back, w1[0, s], 1, 1)
        first_part[0, s] = dot(tok[0, :, columns(d)], back, 0, 0).astype(bf16)
        return carry

    def dead(s, carry):
        first_part[0, s] = jnp.zeros((BLK, BLK), bf16)
        return carry

    count = tab[t, 0, SLOTS]
    lax.fori_loop(0, count, step, 0)
    lax.fori_loop(count, SLOTS, dead, 0)
    in_part[0] = out[...].astype(bf16)


ANY = pl.BlockSpec(memory_space=pl.ANY)
VMEM = pl.BlockSpec(memory_space=pltpu.VMEM)
SMEM = pl.BlockSpec(memory_space=pltpu.SMEM)
HIDDEN = (HIDDEN_BLOCKS, ROWS, BLK)
TILE = (SLOTS, BLK, BLK)
MODEL = (4, ROWS, WIDTH)
DMA = pltpu.SemaphoreType.DMA


def shape(dims, kind=bf16):
    return jax.ShapeDtypeStruct(dims, kind)


def whole(dims):
    return pl.BlockSpec(dims, lambda t: (0,) * len(dims))


def one_of(dims):
    return pl.BlockSpec((1,) + dims, lambda t: (t,) + (0,) * len(dims))


def talk(number, mib=16):
    return pltpu.CompilerParams(collective_id=number, has_side_effects=True, vmem_limit_bytes=mib * MIB)


def compute(kernel, in_specs, out_specs, out_shape, scratch, *args):
    return pl.pallas_call(
        kernel, grid=(4,), in_specs=in_specs, out_specs=out_specs, out_shape=out_shape, scratch_shapes=scratch,
        compiler_params=pltpu.CompilerParams(vmem_limit_bytes=56 * MIB, dimension_semantics=("arbitrary",)),
    )(*args)


def reduce_scratch():
    return [
        pltpu.VMEM((2, 4, BLK, BLK), bf16),
        pltpu.VMEM((2, 2, 4, BLK, BLK), bf16),
        pltpu.VMEM((4, 256, WIDTH), bf16),
        pltpu.VMEM((2, 4, 32, WIDTH), bf16),
        pltpu.VMEM((2, 2, 4, 32, WIDTH), bf16),
    ]


def per_device(tokens, w1_blocks, w2_blocks, block_places, counts, cotangent):
    w1, w2 = w1_blocks[0, 0], w2_blocks[0, 0]
    row = jnp.concatenate([block_places[0, 0], counts[0], jnp.zeros((128 - SLOTS - 1,), jnp.int32)])
    table = jnp.broadcast_to(row[None], (8, 128))

    tok_all, cot_all, w1_all, tab_all = pl.pallas_call(
        gather_kernel,
        out_shape=(shape(MODEL), shape(MODEL), shape((4,) + TILE), shape((4, 8, 128), jnp.int32)),
        in_specs=[ANY] * 4, out_specs=[ANY] * 4,
        scratch_shapes=[DMA((40,)), DMA((40,)), DMA((4,))],
        compiler_params=talk(0),
    )(tokens, cotangent, w1, table)

    hidden_part = compute(
        hidden_kernel, [SMEM, one_of((ROWS, WIDTH)), one_of(TILE)], whole(HIDDEN), shape(HIDDEN),
        [pltpu.VMEM(HIDDEN, f32)], tab_all, tok_all, w1_all,
    )

    w2_all, hidden_other = pl.pallas_call(
        second_kernel,
        out_shape=(shape((4,) + TILE), shape(HIDDEN)),
        in_specs=[ANY] * 2, out_specs=[ANY] * 2,
        scratch_shapes=[DMA((10,)), DMA((10,)), DMA((1,))],
        compiler_params=talk(1),
    )(w2, hidden_part)

    grad_part, out_part, second_part, slope = compute(
        forward_kernel,
        [SMEM, whole(HIDDEN), whole(HIDDEN), one_of((ROWS, WIDTH)), one_of(TILE)],
        [whole(HIDDEN), one_of((ROWS, WIDTH)), one_of(TILE), whole(HIDDEN)],
        (shape(HIDDEN), shape(MODEL), shape((4,) + TILE), shape(HIDDEN, f32)),
        [pltpu.VMEM(HIDDEN, bf16), pltpu.VMEM(HIDDEN, f32), pltpu.VMEM((ROWS, WIDTH), f32)],
        tab_all, hidden_part, hidden_other, cot_all, w2_all,
    )

    grad_other, second_grad, out_mid = pl.pallas_call(
        reduce_kernel,
        out_shape=(shape(HIDDEN), shape(TILE), shape((4, 64, WIDTH))),
        in_specs=[ANY, VMEM, VMEM], out_specs=[ANY, VMEM, VMEM],
        scratch_shapes=reduce_scratch() + [DMA((20,)), DMA((20,))],
        compiler_params=talk(2, 40),
    )(grad_part, second_part, out_part)

    in_part, first_part = compute(
        backward_kernel,
        [SMEM, whole(HIDDEN), whole(HIDDEN), whole(HIDDEN), one_of((ROWS, WIDTH)), one_of(TILE)],
        [one_of((ROWS, WIDTH)), one_of(TILE)],
        (shape(MODEL), shape((4,) + TILE)),
        [pltpu.VMEM(HIDDEN, bf16), pltpu.VMEM((ROWS, WIDTH), f32)],
        tab_all, grad_part, grad_other, slope, tok_all, w1_all,
    )

    first_grad, output, input_grad = pl.pallas_call(
        last_kernel,
        out_shape=(shape(TILE), shape((128, WIDTH)), shape((128, WIDTH))),
        in_specs=[VMEM] * 3, out_specs=[VMEM, ANY, ANY],
        scratch_shapes=reduce_scratch()
        + [pltpu.VMEM((4, 64, WIDTH), bf16)] + [pltpu.VMEM((4, 32, WIDTH), bf16)] * 2
        + [DMA((24,)), DMA((24,)), DMA((2,))],
        compiler_params=talk(3, 40),
    )(first_part, in_part, out_mid)
    return (output, input_grad, first_grad[None, None], second_grad[None, None])


def solution(mesh):
    return jax.shard_map(
        per_device,
        mesh=mesh,
        in_specs=(
            P("col", "row"),
            P("row", "col", None, None, None),
            P("col", "row", None, None, None),
            P("row", "col", None),
            P("row", "col"),
            P("col", "row"),
        ),
        out_specs=(
            P("col", "row"),
            P("col", "row"),
            P("row", "col", None, None, None),
            P("col", "row", None, None, None),
        ),
        check_vma=False,
    )
```

time: 1020 us -> 267 us (0.26)
  waiting for transfers between devices: 818 us -> 0 us
  Pallas kernels: 0 us -> 234 us
  matrix products: 58.8 us -> 0 us
  loops' own time: 39.6 us -> 0 us
  other arithmetic: 35.8 us -> 0.73 us
  local copies, waits for them, and re-layouts: 46.5 us -> 29.4 us
  between operations: 14.2 us -> 1.37 us
    reduce_scatter x4 -> x0, waiting for transfers between devices: 426 us -> none  [the longest x1 172 us: per_device(): lax.psum_scatter(grad_part.astype(jnp.bfloat16), 'row', scatter_dimension...]
    all_gather x4 -> x0, waiting for transfers between devices: 390 us -> none  [the longest x1 169 us: per_device(): lax.all_gather((grad_rows * gelu_slope).astype(jnp.bfloat16), 'row', axis...]
    pallas_call x0 -> x7, Pallas kernels: none -> 234 us  [the longest x1 48.9 us: per_device(): pl.pallas_call(gather_kernel, out_shape=(shape(MODEL), shape(MODEL), shap...]
    dot_general x18 -> x0, matrix products: 58.8 us -> none  [the longest x6 23.3 us: local_advance(): jnp.dot(columns, weights[slot], preferred_element_type=jnp.float32)]
    another operation x6 -> x0, loops' own time: 39.6 us -> none  [the longest x4 26.4 us: local_sum(): return lax.fori_loop(0, count, local_advance, start)]
    convert_element_type x5 -> x0, other arithmetic: 35.1 us -> none  [the longest x1 9.24 us: per_device(): hidden_part.astype(jnp.bfloat16)]
    unnamed x4 -> x38, local copies, waits for them, and re-layouts: 0.89 us -> 29.4 us
    another operation x6 -> x0, local copies, waits for them, and re-layouts: 24.5 us -> none
  transfers between devices with their start and end apart: 8 -> 0, of which waited for: 8 -> 0; matrix products, arithmetic and copies ran while one was open for 13% -> 0% of each run, Pallas kernels for 0% -> 0%
where the time goes in v1:
time: 267 us; the launch traced here: 266 us
  Pallas kernels  234 us (88%)
  local copies, waits for them, and re-layouts  29.4 us (11%)
    pallas_call x1, Pallas kernels, per_device(): pl.pallas_call(gather_kernel, out_shape=(shape(MODEL), shape(MODEL), shap...  48.9 us
    pallas_call x1, Pallas kernels, per_device(): pl.pallas_call(second_kernel, out_shape=(shape((4,) + TILE), shape(HIDDEN...  48.5 us
    pallas_call x1, Pallas kernels, per_device(): pl.pallas_call(reduce_kernel, out_shape=(shape(HIDDEN), shape(TILE), shap...  47.5 us
    pallas_call x3, Pallas kernels, compute(): pl.pallas_call(kernel, grid=(4,), in_specs=in_specs, out_specs=out_specs,...  46.8 us
    pallas_call x1, Pallas kernels, per_device(): pl.pallas_call(last_kernel, out_shape=(shape(TILE), shape((128, WIDTH)),...  42.8 us
    unnamed x38, local copies, waits for them, and re-layouts  29.4 us

profile of v1, /device:TPU:0, one launch (start us, length us, event | category | flops | bytes accessed | tf_op | source)
XLA Modules:
  0.0 266.0 jit_solution(4852750320441356849)
XLA Ops:
  2.0 1.2 copy-done.13
  3.3 0.9 copy-done.14
  4.2 0.9 copy-done.15
  5.2 48.9 %shard_map.93 = (bf16[4,512,1024]{2,1,0:T(8,128)(2,1)S(1)}, bf16[4,512,1024]{2,1,0:T(8,128)(2,1)S(1)}, bf16[4,8,256,256]{3,2,1,0:T(8,128)(2,1)S(1)}, s32[4,8,128]{2,1,0:T(8,128)S(1)}) custom-call(bf16[128,1024]{1,0:T(8,128)(2,1)S(1)} %copy-done.14, bf16[128,1024]{1,0:T(8,128)(2,1)S(1)} %copy-done.15, bf16[8,256,256]{2,1,0:T(8,128)(2,1)S(1)} %bitcast.8, ...), custom_call_target="tpu_custom_call" | custom-call | tf_op jit(solution)/shard_map/pallas_call | solution.py:490
  54.0 1.9 copy-done.1
  56.0 2.0 copy-done.2
  58.0 1.9 copy-done.4
  60.5 9.2 %shard_map.94.part.mine = bf16[8,512,256]{2,1,0:T(8,128)(2,1)} custom-call(s32[4,8,128]{2,1,0:T(8,128)} %copy-done.16, bf16[4,512,1024]{2,1,0:T(8,128)(2,1)} %copy-done.1, bf16[4,8,256,256]{3,2,1,0:T(8,128)(2,1)} %copy-done.2), custom_call_target="tpu_custom_call" | custom-call | tf_op jit(solution)/shard_map/pallas_call | solution.py:469
  69.7 1.6 copy-done
  71.3 48.5 %shard_map.95 = (bf16[4,8,256,256]{3,2,1,0:T(8,128)(2,1)S(1)}, bf16[8,512,256]{2,1,0:T(8,128)(2,1)S(1)}) custom-call(bf16[8,256,256]{2,1,0:T(8,128)(2,1)S(1)} %bitcast.7, bf16[8,512,256]{2,1,0:T(8,128)(2,1)S(1)} %copy-done), custom_call_target="tpu_custom_call" | custom-call | tf_op jit(solution)/shard_map/pallas_call | solution.py:503
  119.8 1.9 copy-done.9
  121.7 1.3 copy-done.11
  123.0 21.1 %shard_map.96 = (bf16[8,512,256]{2,1,0:T(8,128)(2,1)}, bf16[4,512,1024]{2,1,0:T(8,128)(2,1)}, bf16[4,8,256,256]{3,2,1,0:T(8,128)(2,1)}, f32[8,512,256]{2,1,0:T(8,128)}) custom-call(s32[4,8,128]{2,1,0:T(8,128)} %copy-done.16, bf16[8,512,256]{2,1,0:T(8,128)(2,1)} %shard_map.94.part.mine, bf16[8,512,256]{2,1,0:T(8,128)(2,1)} %copy-done.11, ...), custom_call_target="tpu_custom_call" | custom-call | tf_op jit(solution)/shard_map/pallas_call | solution.py:469
  144.1 1.6 copy-done.3
  145.7 2.2 copy-done.7
  147.9 2.2 copy-done.8
  150.1 47.5 %shard_map.97 = (bf16[8,512,256]{2,1,0:T(8,128)(2,1)S(1)}, bf16[8,256,256]{2,1,0:T(8,128)(2,1)S(1)}, bf16[4,64,1024]{2,1,0:T(8,128)(2,1)S(1)}) custom-call(bf16[8,512,256]{2,1,0:T(8,128)(2,1)S(1)} %copy-done.3, bf16[4,8,256,256]{3,2,1,0:T(8,128)(2,1)S(1)} %copy-done.8, bf16[4,512,1024]{2,1,0:T(8,128)(2,1)S(1)} %copy-done.7), custom_call_target="tpu_custom_call" | custom-call | tf_op jit(solution)/shard_map/pallas_call | solution.py:520
  197.6 1.3 copy-done.10
  199.0 16.5 %shard_map.98 = (bf16[4,512,1024]{2,1,0:T(8,128)(2,1)}, bf16[4,8,256,256]{3,2,1,0:T(8,128)(2,1)}) custom-call(s32[4,8,128]{2,1,0:T(8,128)} %copy-done.16, bf16[8,512,256]{2,1,0:T(8,128)(2,1)} %get-tuple-element.28.grad_part.mine, bf16[8,512,256]{2,1,0:T(8,128)(2,1)} %copy-done.10, f32[8,512,256]{2,1,0:T(8,128)} %get-tuple-element.32.slope, ...), custom_call_target="tpu_custom_call" | custom-call | tf_op jit(solution)/shard_map/pallas_call | solution.py:469
  215.5 2.2 copy-done.5
  217.7 2.2 copy-done.6
  219.8 42.8 %shard_map.99 = (bf16[8,256,256]{2,1,0:T(8,128)(2,1)S(1)}, bf16[128,1024]{1,0:T(8,128)(2,1)S(1)}, bf16[128,1024]{1,0:T(8,128)(2,1)S(1)}) custom-call(bf16[4,8,256,256]{3,2,1,0:T(8,128)(2,1)S(1)} %copy-done.6, bf16[4,512,1024]{2,1,0:T(8,128)(2,1)S(1)} %copy-done.5, bf16[4,64,1024]{2,1,0:T(8,128)(2,1)S(1)} %get-tuple-element.35.out_mid), custom_call_target="tpu_custom_call" | custom-call | tf_op jit(solution)/shard_map/pallas_call | solution.py:537
  264.1 1.0 copy.17
  265.0 1.0 copy.18
  (24 shorter events, 2.8 us)
Async XLA Ops:
  2.0 1.2 copy-start.13
  3.3 0.9 copy-start.14
  4.2 0.9 copy-start.15
  54.0 1.9 copy-start.1
  56.0 2.0 copy-start.2
  58.0 1.9 copy-start.4
  59.9 0.6 copy-start.16
  60.5 9.2 %copy-start.12 = (bf16[1,1,8,256,256]{4,3,2,1,0:T(8,128)(2,1)S(1)}, bf16[1,1,8,256,256]{4,3,2,1,0:T(8,128)(2,1)}, u32[]{:S(2)}) copy-start(bf16[1,1,8,256,256]{4,3,2,1,0:T(8,128)(2,1)} %param.8) | copy-start | bytes 3145732
  69.7 1.6 copy-start
  119.8 1.9 copy-start.9
  121.7 1.3 copy-start.11
  144.1 1.6 copy-start.3
  145.7 2.2 copy-start.7
  147.9 2.2 copy-start.8
  197.6 1.3 copy-start.10
  215.5 2.2 copy-start.5
  217.7 2.2 copy-start.6

commit v2 on v0

v2 whole, which is shorter than its diff:
```python
import functools
import math

import jax
import jax.numpy as jnp
from jax import lax
from jax.experimental import pallas as pl
from jax.experimental.pallas import tpu as pltpu
from jax.sharding import PartitionSpec as P

BLK = 256
SLOTS = 8
HIDDEN_BLOCKS = 8
QUARTER = 32
WIDTH = 1024
ROWS = 512
bf16 = jnp.bfloat16
f32 = jnp.float32

gelu_scale = math.sqrt(2.0 / math.pi)
gelu_cubic = 0.044715
MIB = 1 << 20


def gelu_pair(hidden):
    inner = gelu_scale * (hidden + gelu_cubic * hidden * hidden * hidden)
    tanh_value = jnp.tanh(inner)
    value = 0.5 * hidden * (1.0 + tanh_value)
    slope = 0.5 * (1.0 + tanh_value) + 0.5 * hidden * (
        1.0 - tanh_value * tanh_value
    ) * gelu_scale * (1.0 + 3.0 * gelu_cubic * hidden * hidden)
    return (value, slope)


def y_index():
    return lax.div(lax.axis_index("row"), 2)


def peer(dx=0, dy=0, zl=0, zh=0, core=0):
    k, j = lax.axis_index("row"), lax.axis_index("col")
    row = lax.rem(lax.div(k, 2) + dy, 4) * 2 + lax.rem(lax.rem(k, 2) + zl, 2)
    col = (
        lax.rem(lax.div(j, 4) + dx, 4) * 4
        + lax.rem(lax.rem(lax.div(j, 2), 2) + zh, 2) * 2
        + lax.rem(lax.rem(j, 2) + core, 2)
    )
    return (row, col)


Y_PEERS = [dict(dy=1), dict(dy=2), dict(dy=3)]
X_PEERS = [dict(dx=1), dict(dx=3)]
CORE_PEER, ZH_PEER, ZL_PEER = dict(core=1), dict(zh=1), dict(zl=1)


def greet(peers):
    barrier = pltpu.get_barrier_semaphore()
    for one in peers:
        pl.semaphore_signal(barrier, inc=1, device_id=peer(**one), device_id_type=pl.DeviceIdType.MESH)
    pl.semaphore_wait(barrier, len(peers))


class Copies:
    def __init__(self, send, recv):
        self.send, self.recv, self.made, self.done = send, recv, [], set()

    def start(self, src, dst, **to):
        n = len(self.made)
        copy = pltpu.make_async_remote_copy(
            src_ref=src, dst_ref=dst, send_sem=self.send.at[n], recv_sem=self.recv.at[n],
            device_id=peer(**to), device_id_type=pl.DeviceIdType.MESH,
        )
        copy.start()
        self.made.append(copy)
        return copy

    def sent(self, *some):
        for copy in some:
            copy.wait_send()
            self.done.add(id(copy))

    def finish(self):
        for copy in self.made:
            if id(copy) not in self.done:
                copy.wait_send()


def span(start, size):
    return pl.ds(start, size)


LO, HI = span(0, 4), span(4, 4)


class WeightGather:
    def __init__(self, copies, own, slots):
        self.copies, self.own, self.slots = copies, own, slots

    def start(self):
        begin, own, slots = self.copies.start, self.own, self.slots
        self.up_lo = begin(own.at[LO], slots[3].at[LO], dy=1)
        self.down_hi = begin(own.at[HI], slots[1].at[HI], dy=3)
        self.up_hi = begin(own.at[HI], slots[3].at[HI], dy=1)
        self.down_lo = begin(own.at[LO], slots[1].at[LO], dy=3)

    def forward(self):
        self.up_lo.wait_recv()
        self.on_up = self.copies.start(self.slots[3].at[LO], self.slots[2].at[LO], dy=1)
        self.down_hi.wait_recv()
        self.on_down = self.copies.start(self.slots[1].at[HI], self.slots[2].at[HI], dy=3)

    def wait(self, r):
        for copy in {3: (self.up_hi,), 1: (self.down_lo,), 2: (self.on_up, self.on_down)}[r]:
            copy.wait_recv()


def part(core, x, zh, count=1):
    return (slice(None), slice(None), span(((core * 4 + x) * 2 + zh) * QUARTER, count * QUARTER))


def block(d):
    return span(d * BLK, BLK)


class RowGather:
    def __init__(self, copies, own, dest, local):
        self.copies, self.own, self.dest = copies, own, dest
        rows = pl.ds(pl.multiple_of(y_index() * QUARTER, QUARTER), QUARTER)
        self.mine = [
            pltpu.make_async_copy(own.at[rows, block(d)], dest.at[0, d, span(0, QUARTER)], local.at[d])
            for d in range(4)
        ]
        for copy in self.mine:
            copy.start()

    def spread(self):
        self.spread_copies = []
        for r in (1, 3, 2):
            rows = pl.ds(pl.multiple_of(lax.rem(y_index() + r, 4) * QUARTER, QUARTER), QUARTER)
            for d in range(4):
                self.spread_copies.append(self.copies.start(
                    self.own.at[rows, block(d)], self.dest.at[4 - r, d, span(0, QUARTER)], dy=r))

    def both_ways(self, zh):
        own = self.dest.at[part(0, 0, zh)]
        return (
            self.copies.start(own, self.dest.at[part(0, 3, zh)], dx=1),
            self.copies.start(own, self.dest.at[part(0, 1, zh)], dx=3),
        )

    def over(self, x):
        return self.copies.start(self.dest.at[part(0, x, 0, 2)], self.dest.at[part(1, x, 0, 2)], core=1)

    def across(self):
        for copy in self.mine:
            copy.wait()
        for copy in self.spread_copies:
            copy.wait_recv()
        self.across_copy = self.copies.start(self.dest.at[part(0, 0, 0)], self.dest.at[part(0, 0, 1)], zh=1)
        self.first = self.both_ways(0)

    def second(self):
        self.across_copy.wait_recv()
        self.next = self.both_ways(1)
        self.overs = [self.over(0)]

    def onward(self):
        self.first[0].wait_recv()
        self.on_up = self.copies.start(self.dest.at[part(0, 3, 0)], self.dest.at[part(0, 2, 0)], dx=1)
        self.next[1].wait_recv()
        self.on_down = self.copies.start(self.dest.at[part(0, 1, 1)], self.dest.at[part(0, 2, 1)], dx=3)

    def over_near(self):
        self.next[0].wait_recv()
        self.overs.append(self.over(3))
        self.first[1].wait_recv()
        self.overs.append(self.over(1))

    def over_far(self):
        self.on_up.wait_recv()
        self.on_down.wait_recv()
        self.overs.append(self.over(2))

    def finish(self):
        for copy in self.overs:
            copy.wait_recv()


def add_into(dst, *terms):
    def step(n, carry):
        total = terms[0][n].astype(f32)
        for term in terms[1:]:
            total = total + term[n].astype(f32)
        dst[n] = total.astype(dst.dtype)
        return carry

    lax.fori_loop(0, dst.shape[0], step, 0)


class RingReduce:
    def __init__(self, copies, part, far, near, axis):
        self.copies, self.part, self.far, self.near = copies, part, far, near
        self.up, self.down = {axis: 1}, {axis: 3}

    def start_far(self, h):
        way = (self.up, self.down)[h]
        copy = self.copies.start(self.part(2, h), self.far.at[h], **way)
        if h == 0:
            self.far_up = copy
        else:
            self.far_down = copy

    def start_near(self, h):
        if h == 0:
            self.near_up = self.copies.start(self.part(1, 1), self.near.at[0, 1], **self.up)
        else:
            self.near_down = self.copies.start(self.part(3, 0), self.near.at[1, 0], **self.down)

    def onward(self):
        self.far_up.wait_recv()
        add_into(self.far.at[0], self.far.at[0], self.part(1, 0))
        self.last_up = self.copies.start(self.far.at[0], self.near.at[0, 0], **self.up)
        self.far_down.wait_recv()
        add_into(self.far.at[1], self.far.at[1], self.part(3, 1))
        self.last_down = self.copies.start(self.far.at[1], self.near.at[1, 1], **self.down)

    def finish(self, dst):
        for copy in (self.near_up, self.near_down, self.last_up, self.last_down):
            copy.wait_recv()
        for h in range(2):
            add_into(dst(h), self.part(0, h), self.near.at[0, h], self.near.at[1, h])


def weight_part(partial):
    return lambda r, h: partial.at[r, (LO, HI)[h]]


class OutputReduce:
    def __init__(self, copies, partial, arrived, far, near):
        self.copies, self.partial, self.arrived, self.over = copies, partial, arrived, []
        self.ring = RingReduce(copies, lambda r, h: arrived.at[:, span(r * 64 + h * 32, 32)], far, near, "dx")

    def start(self, t):
        self.over.append(self.copies.start(self.partial.at[t, span(256, 256)], self.arrived.at[t], core=1))

    def join(self, r):
        rows = span(64 * r, 64)
        add_into(self.arrived.at[:, rows], self.arrived.at[:, rows], self.partial.at[:, rows])

    def begin_ring(self):
        for copy in self.over:
            copy.wait_recv()
        self.join(2)
        self.ring.start_far(0)
        self.ring.start_far(1)
        self.join(1)
        self.ring.start_near(0)
        self.join(3)
        self.ring.start_near(1)
        self.join(0)


class Home:
    def __init__(self, copies, mid, arrived, output, local):
        self.copies, self.mid, self.arrived, self.output, self.local = copies, mid, arrived, output, local

    def start(self):
        self.over = self.copies.start(self.mid.at[:, span(32, 32)], self.arrived, zh=1)

    def send(self):
        self.over.wait_recv()
        add_into(self.arrived, self.arrived, self.mid.at[:, span(0, 32)])
        rows = pl.ds(pl.multiple_of(y_index() * QUARTER, QUARTER), QUARTER)
        self.mine = pltpu.make_async_copy(self.arrived.at[0], self.output.at[rows], self.local)
        self.mine.start()
        self.sent = [self.copies.start(self.arrived.at[r], self.output.at[rows], dy=r) for r in (2, 1, 3)]

    def finish(self):
        self.mine.wait()
        for copy in self.sent:
            copy.wait_recv()


def columns(d):
    return pl.ds(pl.multiple_of(d * BLK, BLK), BLK)


def dot(a, b, da, db):
    return lax.dot_general(a, b, (((da,), (db,)), ((), ())), preferred_element_type=f32)


def tile_sum(rows, weights, tab, t, h, flipped):
    total = None
    for d in range(4):
        product = dot(rows[t, d], weights[t][tab[t, 0, d * HIDDEN_BLOCKS + h]], 1, int(flipped))
        total = product if total is None else total + product
    return total


def add_tile(rows, weights, tab, t, total, flipped, begin=False):
    def step(h, carry):
        if begin:
            total[h] = tile_sum(rows, weights, tab, t, h, flipped)
        else:
            total[h] += tile_sum(rows, weights, tab, t, h, flipped)
        return carry

    lax.fori_loop(0, HIDDEN_BLOCKS, step, 0)


def last_tile(rows, weights, tab, t, total, flipped, result, first, count):
    def step(h, carry):
        result[h] = (total[h] + tile_sum(rows, weights, tab, t, h, flipped)).astype(bf16)
        return carry

    lax.fori_loop(first, first + count, step, 0)


def model_tile(hidden, weights, tab, t, result, flipped):
    def step(d, carry):
        total = None
        for h in range(HIDDEN_BLOCKS):
            product = dot(hidden[h], weights[t][tab[t, 0, d * HIDDEN_BLOCKS + h]], 1, int(flipped))
            total = product if total is None else total + product
        result[t, :, columns(d)] = total.astype(bf16)
        return carry

    lax.fori_loop(0, 4, step, 0)


def slot_grads(tab, t, first, hidden, rows, result, hidden_left):
    def step(s, carry):
        live = tab[t, 0, 48 + s].astype(f32)
        left, right = hidden[tab[t, 0, 40 + s]], rows[t, tab[t, 0, 32 + s]]
        if not hidden_left:
            left, right = right, left
        result[t, s] = (dot(left, right, 0, 0) * live).astype(bf16)
        return carry

    lax.fori_loop(first, first + 4, step, 0)


CHUNK = 64
CHUNKS = ROWS // CHUNK


def over_chunks(first, count, work):
    def step(n, carry):
        work(first + lax.div(n, CHUNKS), pl.ds(pl.multiple_of(lax.rem(n, CHUNKS) * CHUNK, CHUNK), CHUNK))
        return carry

    lax.fori_loop(0, count * CHUNKS, step, 0)


def layer_kernel(tok, cot, w1, w2, tab_in, output, input_grad, first_grad, second_grad,
                 tok_all, cot_all, w1_0, w1_1, w1_2, w1_3, w2_0, w2_1, w2_2, w2_3,
                 total, hid, hid_other, grad, grad_other, act, model_part, second_part, first_part,
                 far_s, near_s, far_f, near_f, arrived_o, far_o, near_o, arrived_i, far_i, near_i,
                 mid_o, mid_i, home_o, home_i, tab_all, tab, send, recv, local):
    greet(Y_PEERS + X_PEERS + [CORE_PEER, ZH_PEER, ZL_PEER])
    copies = Copies(send, recv)
    first_w, second_w = (w1_0, w1_1, w1_2, w1_3), (w2_0, w2_1, w2_2, w2_3)
    tokens = RowGather(copies, tok, tok_all, local.at[span(14, 4)])
    tab_mine = pltpu.make_async_copy(tab_in, tab_all.at[0], local.at[1])
    tab_mine.start()
    w1_mine = pltpu.make_async_copy(w1, w1_0.at[span(0, SLOTS)], local.at[2])
    w1_mine.start()
    tokens.spread()
    tabs = [copies.start(tab_in, tab_all.at[4 - r], dy=r) for r in (1, 2, 3)]
    w1_ring = WeightGather(copies, w1, first_w)
    w1_ring.start()
    cotangent = RowGather(copies, cot, cot_all, local.at[span(10, 4)])
    w2_mine = pltpu.make_async_copy(w2, w2_0.at[span(0, SLOTS)], local.at[4])
    w2_mine.start()
    for weights in first_w + second_w:
        weights[SLOTS] = jnp.zeros((BLK, BLK), bf16)
    tokens.across()
    cotangent.spread()
    tokens.second()
    tokens.onward()
    w1_ring.forward()
    tokens.over_near()
    tokens.over_far()
    cotangent.across()
    for copy in tabs:
        copy.wait_recv()
    tab_mine.wait()
    tab_down = pltpu.make_async_copy(tab_all, tab, local.at[5])
    tab_down.start()
    tab_down.wait()
    tokens.finish()
    w1_mine.wait()

    add_tile(tok_all, first_w, tab, 0, total, False, True)
    cotangent.second()
    w1_ring.wait(3)
    add_tile(tok_all, first_w, tab, 3, total, False)
    w1_ring.wait(1)
    add_tile(tok_all, first_w, tab, 1, total, False)
    cotangent.onward()
    w1_ring.wait(2)
    w2_ring = WeightGather(copies, w2, second_w)
    w2_ring.start()
    swaps = []
    for n in range(4):
        last_tile(tok_all, first_w, tab, 2, total, False, hid, 2 * n, 2)
        pair = span(2 * n, 2)
        swaps.append(copies.start(hid.at[pair], hid_other.at[pair], zl=1))
    cotangent.over_near()
    cotangent.over_far()
    cotangent.finish()
    w2_mine.wait()

    add_tile(cot_all, second_w, tab, 0, total, True, True)
    w2_ring.forward()
    w2_ring.wait(3)
    add_tile(cot_all, second_w, tab, 3, total, True)
    w2_ring.wait(1)
    add_tile(cot_all, second_w, tab, 1, total, True)
    w2_ring.wait(2)
    last_tile(cot_all, second_w, tab, 2, total, True, grad, 0, HIDDEN_BLOCKS)

    def activate(h, rows):
        value, slope = gelu_pair(hid[h, rows].astype(f32) + hid_other[h, rows].astype(f32))
        act[h, rows] = value.astype(bf16)
        total[h, rows] = slope

    back = []
    for n in range(4):
        swaps[n].wait_recv()
        for m in {2: (0,), 3: (1, 2, 3)}.get(n, ()):
            pair = span(2 * m, 2)
            back.append(copies.start(grad.at[pair], grad_other.at[pair], zl=1))
        over_chunks(2 * n, 2, activate)

    seconds = RingReduce(copies, weight_part(second_part), far_s, near_s, "dy")

    def make_second(t, first):
        slot_grads(tab, t, first, act, cot_all, second_part, True)

    def ring_of(ring, make):
        make(2, 0)
        ring.start_far(0)
        make(2, 4)
        ring.start_far(1)
        make(1, 4)
        ring.start_near(0)
        make(3, 0)
        ring.start_near(1)
        make(1, 0)
        make(3, 4)

    ring_of(seconds, make_second)
    outs = OutputReduce(copies, model_part, arrived_o, far_o, near_o)
    model_tile(act, second_w, tab, 0, model_part, False)
    outs.start(0)
    seconds.onward()
    for t in (1, 2, 3):
        model_tile(act, second_w, tab, t, model_part, False)
        outs.start(t)
    make_second(0, 0)
    make_second(0, 4)
    copies.sent(*swaps)

    def combine(h, rows):
        both = grad[h, rows].astype(f32) + grad_other[h, rows].astype(f32)
        hid[h, rows] = (both * total[h, rows]).astype(bf16)

    back[0].wait_recv()
    over_chunks(0, 2, combine)
    outs.begin_ring()
    back[1].wait_recv()
    over_chunks(2, 2, combine)
    outs.ring.onward()
    back[2].wait_recv()
    over_chunks(4, 2, combine)
    back[3].wait_recv()
    over_chunks(6, 2, combine)

    firsts = RingReduce(copies, weight_part(first_part), far_f, near_f, "dy")

    def make_first(t, first):
        slot_grads(tab, t, first, hid, tok_all, first_part, False)

    ring_of(firsts, make_first)
    outs.ring.finish(lambda h: mid_o.at[:, span(32 * h, 32)])
    out_home = Home(copies, mid_o, home_o, output, local.at[6])
    out_home.start()
    copies.sent(*outs.over)
    ins = OutputReduce(copies, model_part, arrived_i, far_i, near_i)
    model_tile(hid, first_w, tab, 0, model_part, True)
    ins.start(0)
    firsts.onward()
    out_home.send()
    for t in (1, 2, 3):
        model_tile(hid, first_w, tab, t, model_part, True)
        ins.start(t)
    seconds.finish(lambda h: second_part.at[0, (LO, HI)[h]])
    second_out = pltpu.make_async_copy(second_part.at[0], second_grad, local.at[7])
    second_out.start()
    ins.begin_ring()
    make_first(0, 0)
    make_first(0, 4)
    ins.ring.onward()
    ins.ring.finish(lambda h: mid_i.at[:, span(32 * h, 32)])
    in_home = Home(copies, mid_i, home_i, input_grad, local.at[8])
    in_home.start()
    in_home.send()
    firsts.finish(lambda h: first_part.at[0, (LO, HI)[h]])
    first_out = pltpu.make_async_copy(first_part.at[0], first_grad, local.at[9])
    first_out.start()
    out_home.finish()
    in_home.finish()
    second_out.wait()
    first_out.wait()
    copies.finish()


ANY = pl.BlockSpec(memory_space=pl.ANY)
HIDDEN = (HIDDEN_BLOCKS, ROWS, BLK)
TILE = (SLOTS, BLK, BLK)
MODEL = (4, ROWS, WIDTH)
DMA = pltpu.SemaphoreType.DMA


def vmem(*dims):
    return pltpu.VMEM(dims, bf16)


def table(block_places, counts):
    places, slots = block_places[0, 0], jnp.arange(SLOTS, dtype=jnp.int32)
    live = (slots < counts[0, 0]).astype(jnp.int32)
    here = (places[None, :] == jnp.arange(32, dtype=jnp.int32)[:, None]).astype(jnp.int32) * live[None, :]
    source = SLOTS + jnp.sum(here * (slots[None, :] - SLOTS), axis=1)
    row = jnp.concatenate(
        [source, places // HIDDEN_BLOCKS, places % HIDDEN_BLOCKS, live, jnp.zeros((128 - 56,), jnp.int32)])
    return jnp.broadcast_to(row[None], (8, 128))


def per_device(tokens, w1_blocks, w2_blocks, block_places, counts, cotangent):
    weight_ring = [vmem(2, 4, BLK, BLK), vmem(2, 2, 4, BLK, BLK)]
    output_ring = [vmem(4, 256, WIDTH), vmem(2, 4, 32, WIDTH), vmem(2, 2, 4, 32, WIDTH)]
    output, input_grad, first_grad, second_grad = pl.pallas_call(
        layer_kernel,
        out_shape=[jax.ShapeDtypeStruct(dims, bf16) for dims in ((128, WIDTH), (128, WIDTH), TILE, TILE)],
        in_specs=[ANY] * 5,
        out_specs=[ANY] * 4,
        scratch_shapes=[vmem(4, 4, ROWS, BLK)] * 2
        + [vmem(SLOTS + 1, BLK, BLK)] * 8
        + [pltpu.VMEM(HIDDEN, f32)] + [vmem(*HIDDEN)] * 5
        + [vmem(*MODEL)] + [vmem(4, *TILE)] * 2
        + weight_ring * 2 + output_ring * 2
        + [vmem(4, 64, WIDTH)] * 2 + [vmem(4, 32, WIDTH)] * 2
        + [pltpu.VMEM((4, 8, 128), jnp.int32), pltpu.SMEM((4, 8, 128), jnp.int32)]
        + [DMA((120,)), DMA((120,)), DMA((18,))],
        compiler_params=pltpu.CompilerParams(
            collective_id=0, has_side_effects=True, vmem_limit_bytes=62 * MIB),
    )(tokens, cotangent, w1_blocks[0, 0], w2_blocks[0, 0], table(block_places, counts))
    return (output, input_grad, first_grad[None, None], second_grad[None, None])


def solution(mesh):
    return jax.shard_map(
        per_device,
        mesh=mesh,
        in_specs=(
            P("col", "row"),
            P("row", "col", None, None, None),
            P("col", "row", None, None, None),
            P("row", "col", None),
            P("row", "col"),
            P("col", "row"),
        ),
        out_specs=(
            P("col", "row"),
            P("col", "row"),
            P("row", "col", None, None, None),
            P("col", "row", None, None, None),
        ),
        check_vma=False,
    )
```

time: 1020 us -> 213 us (0.21)
  waiting for transfers between devices: 818 us -> 0 us
  Pallas kernels: 0 us -> 204 us
  matrix products: 58.8 us -> 0 us
  loops' own time: 39.6 us -> 0 us
  local copies, waits for them, and re-layouts: 46.5 us -> 7.32 us
  other arithmetic: 35.8 us -> 0.11 us
  between operations: 14.2 us -> 1.33 us
    reduce_scatter x4 -> x0, waiting for transfers between devices: 426 us -> none  [the longest x1 172 us: per_device(): lax.psum_scatter(grad_part.astype(jnp.bfloat16), 'row', scatter_dimension...]
    all_gather x4 -> x0, waiting for transfers between devices: 390 us -> none  [the longest x1 169 us: per_device(): lax.all_gather((grad_rows * gelu_slope).astype(jnp.bfloat16), 'row', axis...]
    pallas_call x0 -> x1, Pallas kernels: none -> 204 us  [per_device(): pl.pallas_call(layer_kernel, out_shape=[jax.ShapeDtypeStruct(dims, bf16)...]
    dot_general x18 -> x0, matrix products: 58.8 us -> none  [the longest x6 23.3 us: local_advance(): jnp.dot(columns, weights[slot], preferred_element_type=jnp.float32)]
    another operation x6 -> x0, loops' own time: 39.6 us -> none  [the longest x4 26.4 us: local_sum(): return lax.fori_loop(0, count, local_advance, start)]
    convert_element_type x5 -> x1, other arithmetic: 35.1 us -> 0.01 us  [table(): live = (slots < counts[0, 0]).astype(jnp.int32)]
    another operation x6 -> x0, local copies, waits for them, and re-layouts: 24.5 us -> none
    dynamic_slice x36 -> x0, local copies, waits for them, and re-layouts: 21.2 us -> none  [the longest x12 7.07 us: local_advance(): current = lax.dynamic_slice_in_dim(total, to_blocks[slot] * BLK, BLK, 1)]
  transfers between devices with their start and end apart: 8 -> 0, of which waited for: 8 -> 0; matrix products, arithmetic and copies ran while one was open for 13% -> 0% of each run, Pallas kernels for 0% -> 0%
where the time goes in v2:
time: 213 us; the launch traced here: 212 us
  Pallas kernels  204 us (96%)
  local copies, waits for them, and re-layouts  7.32 us (3%)
    pallas_call x1, Pallas kernels, per_device(): pl.pallas_call(layer_kernel, out_shape=[jax.ShapeDtypeStruct(dims, bf16)...  204 us
    unnamed x10, local copies, waits for them, and re-layouts  6.64 us

profile of v2, /device:TPU:0, one launch (start us, length us, event | category | flops | bytes accessed | tf_op | source)
XLA Modules:
  0.0 212.4 jit_solution(6078026651383334193)
XLA Ops:
  1.3 0.0 copy-start.2
  1.3 0.6 copy-done.2
  1.9 0.1 multiply_reduce_fusion
  2.1 0.1 concatenate.3
  2.1 0.6 broadcast_in_dim.9.tab_in
  2.7 203.7 %shard_map.93 = (bf16[128,1024]{1,0:T(8,128)(2,1)}, bf16[128,1024]{1,0:T(8,128)(2,1)}, bf16[8,256,256]{2,1,0:T(8,128)(2,1)}, bf16[8,256,256]{2,1,0:T(8,128)(2,1)}) custom-call(bf16[128,1024]{1,0:T(8,128)(2,1)} %tok.1, bf16[128,1024]{1,0:T(8,128)(2,1)} %cot.1, bf16[8,256,256]{2,1,0:T(8,128)(2,1)} %bitcast.13, bf16[8,256,256]{2,1,0:T(8,128)(2,1)} %bitcast.14, ...), custom_call_target="tpu_custom_call" | custom-call | tf_op jit(solution)/shard_map/pallas_call | solution.py:542
  206.4 0.0 copy-start.1
  206.4 1.8 copy.15
  208.2 1.7 copy.16
  209.9 0.0 copy-done.1
  209.9 0.0 copy-start
  209.9 1.0 copy.17
  210.8 0.6 copy-done
  211.5 1.0 copy.18
  (5 shorter events, 0.0 us)
Async XLA Ops:
  1.3 0.7 copy-start.2
  206.4 3.4 %copy-start.1 = (bf16[8,256,256]{2,1,0:T(8,128)(2,1)S(1)}, bf16[8,256,256]{2,1,0:T(8,128)(2,1)}, u32[]{:S(2)}) copy-start(bf16[8,256,256]{2,1,0:T(8,128)(2,1)} %get-tuple-element.10) | copy-start | bytes 3145732
  209.9 1.6 copy-start

commit v3 on v2

v3 whole, which is shorter than its diff:
```python
import functools
import math

import jax
import jax.numpy as jnp
from jax import lax
from jax.experimental import pallas as pl
from jax.experimental.pallas import tpu as pltpu
from jax.sharding import PartitionSpec as P

BLK = 256
SLOTS = 8
HIDDEN_BLOCKS = 8
QUARTER = 32
WIDTH = 1024
ROWS = 512
bf16 = jnp.bfloat16
f32 = jnp.float32

gelu_scale = math.sqrt(2.0 / math.pi)
gelu_cubic = 0.044715
MIB = 1 << 20


def gelu_pair(hidden):
    inner = gelu_scale * (hidden + gelu_cubic * hidden * hidden * hidden)
    tanh_value = jnp.tanh(inner)
    value = 0.5 * hidden * (1.0 + tanh_value)
    slope = 0.5 * (1.0 + tanh_value) + 0.5 * hidden * (
        1.0 - tanh_value * tanh_value
    ) * gelu_scale * (1.0 + 3.0 * gelu_cubic * hidden * hidden)
    return (value, slope)


def y_index():
    return lax.div(lax.axis_index("row"), 2)


def peer(dx=0, dy=0, zl=0, zh=0, core=0):
    k, j = lax.axis_index("row"), lax.axis_index("col")
    row = lax.rem(lax.div(k, 2) + dy, 4) * 2 + lax.rem(lax.rem(k, 2) + zl, 2)
    col = (
        lax.rem(lax.div(j, 4) + dx, 4) * 4
        + lax.rem(lax.rem(lax.div(j, 2), 2) + zh, 2) * 2
        + lax.rem(lax.rem(j, 2) + core, 2)
    )
    return (row, col)


Y_PEERS = [dict(dy=1), dict(dy=2), dict(dy=3)]
X_PEERS = [dict(dx=1), dict(dx=3)]
CORE_PEER, ZH_PEER, ZL_PEER = dict(core=1), dict(zh=1), dict(zl=1)


def greet(peers):
    barrier = pltpu.get_barrier_semaphore()
    for one in peers:
        pl.semaphore_signal(barrier, inc=1, device_id=peer(**one), device_id_type=pl.DeviceIdType.MESH)
    pl.semaphore_wait(barrier, len(peers))


class Copies:
    def __init__(self, send, recv):
        self.send, self.recv, self.made, self.done = send, recv, [], set()

    def start(self, src, dst, **to):
        n = len(self.made)
        copy = self.at(n, src, dst, **to)
        copy.start()
        self.made.append(copy)
        return copy

    def reserve(self, count):
        first = len(self.made)
        self.made += [None] * count
        return first

    def at(self, n, src, dst, **to):
        return pltpu.make_async_remote_copy(
            src_ref=src, dst_ref=dst, send_sem=self.send.at[n], recv_sem=self.recv.at[n],
            device_id=peer(**to), device_id_type=pl.DeviceIdType.MESH,
        )

    def sent(self, *some):
        for copy in some:
            copy.wait_send()
            self.done.add(id(copy))

    def finish(self):
        for copy in self.made:
            if copy is not None and id(copy) not in self.done:
                copy.wait_send()


def span(start, size):
    return pl.ds(start, size)


LO, HI = span(0, 4), span(4, 4)


class WeightGather:
    def __init__(self, copies, own, slots):
        self.copies, self.own, self.slots = copies, own, slots

    def start(self):
        begin, own, slots = self.copies.start, self.own, self.slots
        self.up_lo = begin(own.at[LO], slots[3].at[LO], dy=1)
        self.down_hi = begin(own.at[HI], slots[1].at[HI], dy=3)
        self.up_hi = begin(own.at[HI], slots[3].at[HI], dy=1)
        self.down_lo = begin(own.at[LO], slots[1].at[LO], dy=3)

    def forward(self):
        self.up_lo.wait_recv()
        self.on_up = self.copies.start(self.slots[3].at[LO], self.slots[2].at[LO], dy=1)
        self.down_hi.wait_recv()
        self.on_down = self.copies.start(self.slots[1].at[HI], self.slots[2].at[HI], dy=3)

    def wait(self, r):
        for copy in {3: (self.up_hi,), 1: (self.down_lo,), 2: (self.on_up, self.on_down)}[r]:
            copy.wait_recv()


def part(core, x, zh, count=1):
    return (slice(None), slice(None), span(((core * 4 + x) * 2 + zh) * QUARTER, count * QUARTER))


def block(d):
    return span(d * BLK, BLK)


class RowGather:
    def __init__(self, copies, own, dest, local, early=None):
        self.copies, self.own, self.dest, self.local, self.early = copies, own, dest, local, early
        self.overs = []
        if early is not None:
            self.early_copy = copies.start(own, early, zh=1)

    def spread(self):
        self.mine, self.spread_copies = [], []
        sources = [self.own]
        if self.early is not None:
            self.early_copy.wait_recv()
            sources.append(self.early)
        for r in (0, 1, 3, 2):
            rows = pl.ds(pl.multiple_of(lax.rem(y_index() + r, 4) * QUARTER, QUARTER), QUARTER)
            for zh, source in enumerate(sources):
                for d in range(4):
                    piece = source.at[rows, block(d)]
                    place = self.dest.at[(4 - r) % 4, d, span(zh * QUARTER, QUARTER)]
                    if r == 0:
                        copy = pltpu.make_async_copy(piece, place, self.local.at[len(self.mine)])
                        copy.start()
                        self.mine.append(copy)
                    else:
                        self.spread_copies.append(self.copies.start(piece, place, dy=r))

    def wait_spread(self):
        for copy in self.mine:
            copy.wait()
        for copy in self.spread_copies:
            copy.wait_recv()

    def both_ways(self, zh):
        own = self.dest.at[part(0, 0, zh)]
        return (
            self.copies.start(own, self.dest.at[part(0, 3, zh)], dx=1),
            self.copies.start(own, self.dest.at[part(0, 1, zh)], dx=3),
        )

    def over(self, x):
        self.overs.append(
            self.copies.start(self.dest.at[part(0, x, 0, 2)], self.dest.at[part(1, x, 0, 2)], core=1))

    def begin(self):
        self.wait_spread()
        if self.early is None:
            self.across = self.copies.start(self.dest.at[part(0, 0, 0)], self.dest.at[part(0, 0, 1)], zh=1)
            self.first = self.both_ways(0)
        else:
            up_0, down_0 = self.both_ways(0)
            up_1, down_1 = self.both_ways(1)
            self.first, self.next = (up_0, down_0), (up_1, down_1)
            self.over(0)

    def onward_up(self):
        self.first[0].wait_recv()
        self.on_up = self.copies.start(self.dest.at[part(0, 3, 0)], self.dest.at[part(0, 2, 0)], dx=1)

    def second(self):
        self.across.wait_recv()
        self.next = self.both_ways(1)
        self.over(0)

    def onward_down(self):
        self.next[1].wait_recv()
        self.on_down = self.copies.start(self.dest.at[part(0, 1, 1)], self.dest.at[part(0, 2, 1)], dx=3)

    def over_near(self):
        self.next[0].wait_recv()
        self.over(3)
        self.first[1].wait_recv()
        self.over(1)

    def over_far(self):
        self.on_up.wait_recv()
        self.on_down.wait_recv()
        self.over(2)

    def finish(self):
        for copy in self.overs:
            copy.wait_recv()


def add_into(dst, *terms):
    def add(*refs):
        total = refs[1][...].astype(f32)
        for ref in refs[2:]:
            total = total + ref[...].astype(f32)
        refs[0][...] = total.astype(dst.dtype)

    if len(dst.shape) == 2:
        add(dst, *terms)
    else:

        def step(n, carry):
            add(*[ref.at[n] for ref in (dst,) + terms])
            return carry

        lax.fori_loop(0, dst.shape[0], step, 0)


class RingReduce:
    def __init__(self, copies, part, far, near, axis):
        self.copies, self.part, self.far, self.near = copies, part, far, near
        self.up, self.down = {axis: 1}, {axis: 3}

    def start_far(self):
        self.far_up = self.copies.start(self.part(2, 0), self.far.at[0], **self.up)
        self.far_down = self.copies.start(self.part(2, 1), self.far.at[1], **self.down)

    def start_up(self):
        self.near_up = self.copies.start(self.part(1, 1), self.near.at[0, 1], **self.up)

    def start_down(self):
        self.near_down = self.copies.start(self.part(3, 0), self.near.at[1, 0], **self.down)

    def onward(self):
        self.far_up.wait_recv()
        add_into(self.far.at[0], self.far.at[0], self.part(1, 0))
        self.last_up = self.copies.start(self.far.at[0], self.near.at[0, 0], **self.up)
        self.far_down.wait_recv()
        add_into(self.far.at[1], self.far.at[1], self.part(3, 1))
        self.last_down = self.copies.start(self.far.at[1], self.near.at[1, 1], **self.down)

    def finish(self, dst):
        for h, arrivals in enumerate(((self.near_down, self.last_up), (self.near_up, self.last_down))):
            for copy in arrivals:
                copy.wait_recv()
            add_into(dst(h), self.part(0, h), self.near.at[0, h], self.near.at[1, h])


def weight_part(partial):
    return lambda r, h: partial.at[r, (LO, HI)[h]]


class OutputReduce:
    def __init__(self, copies, t, partial, arrived, far, near, mid, home):
        self.copies, self.t, self.partial, self.arrived, self.mid, self.home = copies, t, partial, arrived, mid, home
        self.ring = RingReduce(copies, lambda r, h: arrived.at[span(r * 64 + h * 32, 32)], far, near, "dx")

    def start(self):
        self.over = self.copies.start(self.partial.at[span(256, 256)], self.arrived, core=1)

    def join(self, r):
        rows = span(64 * r, 64)
        add_into(self.arrived.at[rows], self.arrived.at[rows], self.partial.at[rows])

    def begin(self):
        self.over.wait_recv()
        self.join(2)
        self.ring.start_far()
        self.join(1)
        self.ring.start_up()
        self.join(3)
        self.ring.start_down()
        self.join(0)

    def finish(self):
        self.ring.finish(lambda h: self.mid.at[span(32 * h, 32)])

    def across(self):
        self.across_copy = self.copies.start(self.mid.at[span(32, 32)], self.home, zh=1)

    def send_home(self, output, local):
        self.across_copy.wait_recv()
        add_into(self.home, self.home, self.mid.at[span(0, 32)])
        rows = pl.ds(pl.multiple_of(y_index() * QUARTER, QUARTER), QUARTER)
        if self.t == 0:
            self.last = pltpu.make_async_copy(self.home, output.at[rows], local)
            self.last.start()
        else:
            self.last = self.copies.start(self.home, output.at[rows], dy=self.t)

    def arrive(self):
        if self.t == 0:
            self.last.wait()
        else:
            self.last.wait_recv()


def columns(d):
    return pl.ds(pl.multiple_of(d * BLK, BLK), BLK)


def dot(a, b, da, db):
    return lax.dot_general(a, b, (((da,), (db,)), ((), ())), preferred_element_type=f32)


def hidden_block(rows, weights, tab, h, flipped):
    total = None
    for t in range(4):
        for d in range(4):
            weight = weights[t][tab[t, 0, d * HIDDEN_BLOCKS + h]]
            product = dot(rows[t, d], weight, 1, int(flipped))
            total = product if total is None else total + product
    return total.astype(bf16)


def model_tile(hidden, weights, tab, t, result, flipped, blocks, add=False):
    def step(n, carry):
        for d in (2 * n, 2 * n + 1):
            total = result[t, :, columns(d)].astype(f32) if add else None
            for h in blocks:
                product = dot(hidden[h], weights[t][tab[t, 0, d * HIDDEN_BLOCKS + h]], 1, int(flipped))
                total = product if total is None else total + product
            result[t, :, columns(d)] = total.astype(bf16)
        return carry

    lax.fori_loop(0, 2, step, 0)


def slot_grads(tab, t, hidden, rows, result, hidden_left):
    for s in range(SLOTS):
        live = tab[t, 0, 48 + s].astype(f32)
        left, right = hidden[tab[t, 0, 40 + s]], rows[t, tab[t, 0, 32 + s]]
        if not hidden_left:
            left, right = right, left
        result[t, s] = (dot(left, right, 0, 0) * live).astype(bf16)


CHUNK = 64
CHUNKS = ROWS // CHUNK


def over_chunks(h, work):
    def step(n, carry):
        work(h, pl.ds(pl.multiple_of(n * CHUNK, CHUNK), CHUNK))
        return carry

    lax.fori_loop(0, CHUNKS, step, 0)


def layer_kernel(tok, cot, w1, w2, tab_in, output, input_grad, first_grad, second_grad,
                 tok_all, cot_all, w1_0, w1_1, w1_2, w1_3, w2_0, w2_1, w2_2, w2_3,
                 slope_all, hid, hid_other, grad, grad_other, act, model_part, second_part, first_part,
                 far_s, near_s, far_f, near_f, arrived_o, far_o, near_o, mid_o, home_o,
                 arrived_i, far_i, near_i, mid_i, home_i, cot_early, tab_all, tab, send, recv, local):
    greet(Y_PEERS + X_PEERS + [CORE_PEER, ZH_PEER, ZL_PEER])
    copies = Copies(send, recv)
    first_w, second_w = (w1_0, w1_1, w1_2, w1_3), (w2_0, w2_1, w2_2, w2_3)
    tokens = RowGather(copies, tok, tok_all, local.at[span(14, 4)])
    tokens.spread()
    w1_ring = WeightGather(copies, w1, first_w)
    w1_ring.start()
    tabs = [copies.start(tab_in, tab_all.at[4 - r], dy=r) for r in (1, 2, 3)]
    tab_mine = pltpu.make_async_copy(tab_in, tab_all.at[0], local.at[1])
    tab_mine.start()
    w1_mine = pltpu.make_async_copy(w1, w1_0.at[span(0, SLOTS)], local.at[2])
    w1_mine.start()
    w2_mine = pltpu.make_async_copy(w2, w2_0.at[span(0, SLOTS)], local.at[4])
    w2_mine.start()
    for weights in first_w + second_w:
        weights[SLOTS] = jnp.zeros((BLK, BLK), bf16)
    tokens.begin()
    tokens.onward_up()
    tokens.second()
    cotangent = RowGather(copies, cot, cot_all, local.at[span(18, 8)], cot_early)
    w1_ring.forward()
    tokens.onward_down()
    tokens.over_near()
    tokens.over_far()
    for copy in tabs:
        copy.wait_recv()
    tab_mine.wait()
    tab_down = pltpu.make_async_copy(tab_all, tab, local.at[5])
    tab_down.start()
    tab_down.wait()
    tokens.finish()
    w1_mine.wait()
    for r in (3, 1, 2):
        w1_ring.wait(r)
    cotangent.spread()
    w2_ring = WeightGather(copies, w2, second_w)
    w2_ring.start()

    swap = copies.reserve(HIDDEN_BLOCKS)
    back = copies.reserve(HIDDEN_BLOCKS)

    def swap_copy(h):
        return copies.at(swap + h, hid.at[h], hid_other.at[h], zl=1)

    def back_copy(h):
        return copies.at(back + h, grad.at[h], grad_other.at[h], zl=1)

    def make_hidden(h, carry):
        hid[h] = hidden_block(tok_all, first_w, tab, h, False)
        swap_copy(h).start()
        return carry

    lax.fori_loop(0, 4, make_hidden, 0)
    cotangent.begin()
    lax.fori_loop(4, 8, make_hidden, 0)
    cotangent.onward_up()
    w2_ring.forward()
    cotangent.onward_down()

    def activate(h, rows):
        value, slope = gelu_pair(hid[h, rows].astype(f32) + hid_other[h, rows].astype(f32))
        act[h, rows] = value.astype(bf16)
        slope_all[h, rows] = slope

    def activations(*blocks):
        for h in blocks:
            swap_copy(h).wait_recv()
            over_chunks(h, activate)

    activations(0, 1)
    cotangent.over_near()
    cotangent.over_far()
    activations(2, 3)
    cotangent.finish()
    w2_mine.wait()

    def make_grad(h, carry):
        grad[h] = hidden_block(cot_all, second_w, tab, h, True)
        return carry

    for r in (3, 1, 2):
        w2_ring.wait(r)
    lax.fori_loop(0, 4, make_grad, 0)
    activations(4, 5, 6)
    for h in range(4):
        back_copy(h).start()
    activations(7)

    seconds = RingReduce(copies, weight_part(second_part), far_s, near_s, "dy")

    def begin_ring(ring, hidden, rows, result, hidden_left):
        slot_grads(tab, 2, hidden, rows, result, hidden_left)
        ring.start_far()
        slot_grads(tab, 1, hidden, rows, result, hidden_left)
        ring.start_up()
        slot_grads(tab, 3, hidden, rows, result, hidden_left)
        ring.start_down()
        slot_grads(tab, 0, hidden, rows, result, hidden_left)

    def make_rest(h, carry):
        make_grad(h, carry)
        back_copy(h).start()
        return carry

    begin_ring(seconds, act, cot_all, second_part, True)
    lax.fori_loop(4, 8, make_rest, 0)
    order = (2, 1, 3, 0)
    every = tuple(range(HIDDEN_BLOCKS))
    outs = {t: OutputReduce(copies, t, model_part.at[t], arrived_o.at[t], far_o.at[t], near_o.at[t], mid_o.at[t], home_o.at[t])
            for t in order}
    for t in order:
        model_tile(act, second_w, tab, t, model_part, False, every)
        outs[t].start()
    seconds.onward()
    for h in range(HIDDEN_BLOCKS):
        swap_copy(h).wait_send()

    def combine(h, rows):
        both = grad[h, rows].astype(f32) + grad_other[h, rows].astype(f32)
        hid[h, rows] = (both * slope_all[h, rows]).astype(bf16)

    def combined(*blocks):
        for h in blocks:
            back_copy(h).wait_recv()
            over_chunks(h, combine)

    combined(0, 1)
    for t in order:
        outs[t].begin()
    combined(2, 3)
    for t in order:
        outs[t].ring.onward()
    combined(4, 5)

    copies.sent(*[outs[t].over for t in order])
    for t in order:
        model_tile(hid, first_w, tab, t, model_part, True, every[:6])
    combined(6, 7)
    firsts = RingReduce(copies, weight_part(first_part), far_f, near_f, "dy")
    ins = {t: OutputReduce(copies, t, model_part.at[t], arrived_i.at[t], far_i.at[t], near_i.at[t], mid_i.at[t], home_i.at[t])
           for t in order}
    begin_ring(firsts, hid, tok_all, first_part, False)
    for t in order:
        model_tile(hid, first_w, tab, t, model_part, True, every[6:], True)
        ins[t].start()
    for t in order:
        ins[t].begin()
    for t in order:
        outs[t].finish()
        outs[t].across()
    firsts.onward()
    for t in order:
        outs[t].send_home(output, local.at[6])
    for t in order:
        ins[t].ring.onward()
    seconds.finish(lambda h: second_part.at[0, (LO, HI)[h]])
    second_out = pltpu.make_async_copy(second_part.at[0], second_grad, local.at[7])
    second_out.start()
    for t in order:
        ins[t].finish()
        ins[t].across()
    for t in order:
        ins[t].send_home(input_grad, local.at[8])
    firsts.finish(lambda h: first_part.at[0, (LO, HI)[h]])
    first_out = pltpu.make_async_copy(first_part.at[0], first_grad, local.at[9])
    first_out.start()
    for t in order:
        outs[t].arrive()
        ins[t].arrive()
    second_out.wait()
    first_out.wait()
    for h in range(HIDDEN_BLOCKS):
        back_copy(h).wait_send()
    copies.finish()


def place_kernel(*refs):
    for source, dest in zip(refs[:4], refs[4:]):
        dest[...] = source[...]


ANY = pl.BlockSpec(memory_space=pl.ANY)
HIDDEN = (HIDDEN_BLOCKS, ROWS, BLK)
TILE = (SLOTS, BLK, BLK)
MODEL = (4, ROWS, WIDTH)
DMA = pltpu.SemaphoreType.DMA


def vmem(*dims):
    return pltpu.VMEM(dims, bf16)


def table(block_places, counts):
    places, slots = block_places[0, 0], jnp.arange(SLOTS, dtype=jnp.int32)
    live = (slots < counts[0, 0]).astype(jnp.int32)
    here = (places[None, :] == jnp.arange(32, dtype=jnp.int32)[:, None]).astype(jnp.int32) * live[None, :]
    source = SLOTS + jnp.sum(here * (slots[None, :] - SLOTS), axis=1)
    row = jnp.concatenate(
        [source, places // HIDDEN_BLOCKS, places % HIDDEN_BLOCKS, live, jnp.zeros((128 - 56,), jnp.int32)])
    return jnp.broadcast_to(row[None], (8, 128))


def per_device(tokens, w1_blocks, w2_blocks, block_places, counts, cotangent):
    weight_ring = [vmem(2, 4, BLK, BLK), vmem(2, 2, 4, BLK, BLK)]
    output_ring = [vmem(4, 256, WIDTH), vmem(4, 2, 32, WIDTH), vmem(4, 2, 2, 32, WIDTH), vmem(4, 64, WIDTH), vmem(4, 32, WIDTH)]
    shapes = [jax.ShapeDtypeStruct(dims, bf16) for dims in ((128, WIDTH), (128, WIDTH), TILE, TILE)]
    results = pl.pallas_call(
        layer_kernel,
        out_shape=shapes,
        in_specs=[ANY] * 5,
        out_specs=[ANY] * 4,
        scratch_shapes=[vmem(4, 4, ROWS, BLK)] * 2
        + [vmem(SLOTS + 1, BLK, BLK)] * 8
        + [pltpu.VMEM(HIDDEN, f32)] + [vmem(*HIDDEN)] * 5
        + [vmem(*MODEL)] + [vmem(4, *TILE)] * 2
        + weight_ring * 2 + output_ring * 2
        + [vmem(128, WIDTH)]
        + [pltpu.VMEM((4, 8, 128), jnp.int32), pltpu.SMEM((4, 8, 128), jnp.int32)]
        + [DMA((200,)), DMA((200,)), DMA((26,))],
        compiler_params=pltpu.CompilerParams(
            collective_id=0, has_side_effects=True, vmem_limit_bytes=62 * MIB),
    )(tokens, cotangent, w1_blocks[0, 0], w2_blocks[0, 0], table(block_places, counts))
    blocks = [pl.BlockSpec((32, WIDTH), lambda n: (n, 0))] * 2 + [pl.BlockSpec((2, BLK, BLK), lambda n: (n, 0, 0))] * 2
    output, input_grad, first_grad, second_grad = pl.pallas_call(
        place_kernel, grid=(4,), out_shape=shapes, in_specs=blocks, out_specs=blocks,
    )(*results)
    return (output, input_grad, first_grad[None, None], second_grad[None, None])


def solution(mesh):
    return jax.shard_map(
        per_device,
        mesh=mesh,
        in_specs=(
            P("col", "row"),
            P("row", "col", None, None, None),
            P("col", "row", None, None, None),
            P("row", "col", None),
            P("row", "col"),
            P("col", "row"),
        ),
        out_specs=(
            P("col", "row"),
            P("col", "row"),
            P("row", "col", None, None, None),
            P("col", "row", None, None, None),
        ),
        check_vma=False,
    )
```

time: 213 us -> 190 us (0.89)
  Pallas kernels: 204 us -> 187 us
  local copies, waits for them, and re-layouts: 7.32 us -> 1.32 us
    pallas_call x1 -> x2, Pallas kernels: 204 us -> 187 us  [the longest x1 183 us: per_device(): pl.pallas_call(layer_kernel, out_shape=shapes, in_specs=[ANY] * 5, out_sp...]
    unnamed x10 -> x2, local copies, waits for them, and re-layouts: 6.64 us -> 0.64 us
where the time goes in v3:
time: 190 us
  Pallas kernels  187 us (98%)
    pallas_call x1, Pallas kernels, per_device(): pl.pallas_call(layer_kernel, out_shape=shapes, in_specs=[ANY] * 5, out_sp...  183 us
    pallas_call x1, Pallas kernels, per_device(): pl.pallas_call(place_kernel, grid=(4,), out_shape=shapes, in_specs=blocks...  3.99 us

profile of v3, /device:TPU:0, one launch (start us, length us, event | category | flops | bytes accessed | tf_op | source)
XLA Modules:
  0.0 189.7 jit_solution(5491423966844994299)
XLA Ops:
  1.3 0.0 copy-start
  1.3 0.6 copy-done
  1.9 0.1 multiply_reduce_fusion
  2.1 0.1 concatenate.3
  2.1 0.6 broadcast_in_dim.9.tab_in
  2.7 183.0 %shard_map.93 = (bf16[128,1024]{1,0:T(8,128)(2,1)}, bf16[128,1024]{1,0:T(8,128)(2,1)}, bf16[8,256,256]{2,1,0:T(8,128)(2,1)}, bf16[8,256,256]{2,1,0:T(8,128)(2,1)}) custom-call(bf16[128,1024]{1,0:T(8,128)(2,1)} %tok.1, bf16[128,1024]{1,0:T(8,128)(2,1)} %cot.1, bf16[8,256,256]{2,1,0:T(8,128)(2,1)} %bitcast.13, bf16[8,256,256]{2,1,0:T(8,128)(2,1)} %bitcast.14, ...), custom_call_target="tpu_custom_call" | custom-call | tf_op jit(solution)/shard_map/pallas_call | solution.py:575
  185.7 4.0 %shard_map.94 = (bf16[128,1024]{1,0:T(8,128)(2,1)}, bf16[128,1024]{1,0:T(8,128)(2,1)}, bf16[8,256,256]{2,1,0:T(8,128)(2,1)}, bf16[8,256,256]{2,1,0:T(8,128)(2,1)}) custom-call(bf16[128,1024]{1,0:T(8,128)(2,1)} %get-tuple-element.12.refs_0_, bf16[128,1024]{1,0:T(8,128)(2,1)} %get-tuple-element.13.refs_1_, bf16[8,256,256]{2,1,0:T(8,128)(2,1)} %get-tuple-element.14.refs_2_, ...), custom_call_target="tpu_custom_call" | custom-call | tf_op jit(solution)/shard_map/pallas_call | solution.py:592
  (5 shorter events, 0.0 us)
Async XLA Ops:
  1.3 0.7 copy-start

commit v4 on v3

--- a/solution.py
+++ b/solution.py
@@ -63,11 +63,14 @@
     def __init__(self, send, recv):
         self.send, self.recv, self.made, self.done = send, recv, [], set()
 
+    def make(self, src, dst, **to):
+        copy = self.at(len(self.made), src, dst, **to)
+        self.made.append(copy)
+        return copy
+
     def start(self, src, dst, **to):
-        n = len(self.made)
-        copy = self.at(n, src, dst, **to)
+        copy = self.make(src, dst, **to)
         copy.start()
-        self.made.append(copy)
         return copy
 
     def reserve(self, count):
@@ -101,20 +104,23 @@
 
 class WeightGather:
     def __init__(self, copies, own, slots):
-        self.copies, self.own, self.slots = copies, own, slots
+        make = copies.make
+        self.up_lo = make(own.at[LO], slots[3].at[LO], dy=1)
+        self.down_hi = make(own.at[HI], slots[1].at[HI], dy=3)
+        self.up_hi = make(own.at[HI], slots[3].at[HI], dy=1)
+        self.down_lo = make(own.at[LO], slots[1].at[LO], dy=3)
+        self.on_up = make(slots[3].at[LO], slots[2].at[LO], dy=1)
+        self.on_down = make(slots[1].at[HI], slots[2].at[HI], dy=3)
 
     def start(self):
-        begin, own, slots = self.copies.start, self.own, self.slots
-        self.up_lo = begin(own.at[LO], slots[3].at[LO], dy=1)
-        self.down_hi = begin(own.at[HI], slots[1].at[HI], dy=3)
-        self.up_hi = begin(own.at[HI], slots[3].at[HI], dy=1)
-        self.down_lo = begin(own.at[LO], slots[1].at[LO], dy=3)
+        for copy in (self.up_lo, self.down_hi, self.up_hi, self.down_lo):
+            copy.start()
 
     def forward(self):
         self.up_lo.wait_recv()
-        self.on_up = self.copies.start(self.slots[3].at[LO], self.slots[2].at[LO], dy=1)
+        self.on_up.start()
         self.down_hi.wait_recv()
-        self.on_down = self.copies.start(self.slots[1].at[HI], self.slots[2].at[HI], dy=3)
+        self.on_down.start()
 
     def wait(self, r):
         for copy in {3: (self.up_hi,), 1: (self.down_lo,), 2: (self.on_up, self.on_down)}[r]:
@@ -368,11 +374,13 @@
                  arrived_i, far_i, near_i, mid_i, home_i, cot_early, tab_all, tab, send, recv, local):
     greet(Y_PEERS + X_PEERS + [CORE_PEER, ZH_PEER, ZL_PEER])
     copies = Copies(send, recv)
+    core = lax.rem(lax.axis_index("col"), 2)
     first_w, second_w = (w1_0, w1_1, w1_2, w1_3), (w2_0, w2_1, w2_2, w2_3)
     tokens = RowGather(copies, tok, tok_all, local.at[span(14, 4)])
     tokens.spread()
     w1_ring = WeightGather(copies, w1, first_w)
-    w1_ring.start()
+    on_first, on_second = pl.when(core == 0), pl.when(core == 1)
+    on_first(w1_ring.start)
     tabs = [copies.start(tab_in, tab_all.at[4 - r], dy=r) for r in (1, 2, 3)]
     tab_mine = pltpu.make_async_copy(tab_in, tab_all.at[0], local.at[1])
     tab_mine.start()
@@ -384,12 +392,14 @@
         weights[SLOTS] = jnp.zeros((BLK, BLK), bf16)
     tokens.begin()
     tokens.onward_up()
+    on_first(w1_ring.forward)
     tokens.second()
+    on_second(w1_ring.start)
     cotangent = RowGather(copies, cot, cot_all, local.at[span(18, 8)], cot_early)
-    w1_ring.forward()
     tokens.onward_down()
     tokens.over_near()
     tokens.over_far()
+    on_second(w1_ring.forward)
     for copy in tabs:
         copy.wait_recv()
     tab_mine.wait()
@@ -400,9 +410,7 @@
     w1_mine.wait()
     for r in (3, 1, 2):
         w1_ring.wait(r)
-    cotangent.spread()
     w2_ring = WeightGather(copies, w2, second_w)
-    w2_ring.start()
 
     swap = copies.reserve(HIDDEN_BLOCKS)
     back = copies.reserve(HIDDEN_BLOCKS)
@@ -419,6 +427,8 @@
         return carry
 
     lax.fori_loop(0, 4, make_hidden, 0)
+    cotangent.spread()
+    w2_ring.start()
     cotangent.begin()
     lax.fori_loop(4, 8, make_hidden, 0)
     cotangent.onward_up()

time: 190 us -> 183 us (0.963); the launches traced: 190 us -> 180 us
  Pallas kernels: 187 us -> 177 us
    pallas_call x1, Pallas kernels: 183 us -> 173 us  [per_device(): pl.pallas_call(layer_kernel, out_shape=shapes, in_specs=[ANY] * 5, out_sp...]
where the time goes in v4:
time: 183 us; the launch traced here: 180 us
  Pallas kernels  177 us (97%)
    pallas_call x1, Pallas kernels, per_device(): pl.pallas_call(layer_kernel, out_shape=shapes, in_specs=[ANY] * 5, out_sp...  173 us
    pallas_call x1, Pallas kernels, per_device(): pl.pallas_call(place_kernel, grid=(4,), out_shape=shapes, in_specs=blocks...  3.99 us

profile of v4, /device:TPU:0, one launch (start us, length us, event | category | flops | bytes accessed | tf_op | source)
XLA Modules:
  0.0 179.5 jit_solution(6866445701353689184)
XLA Ops:
  1.3 0.0 copy-start
  1.3 0.6 copy-done
  1.9 0.1 multiply_reduce_fusion
  2.1 0.1 concatenate.3
  2.1 0.6 broadcast_in_dim.9.tab_in
  2.7 172.8 %shard_map.93 = (bf16[128,1024]{1,0:T(8,128)(2,1)}, bf16[128,1024]{1,0:T(8,128)(2,1)}, bf16[8,256,256]{2,1,0:T(8,128)(2,1)}, bf16[8,256,256]{2,1,0:T(8,128)(2,1)}) custom-call(bf16[128,1024]{1,0:T(8,128)(2,1)} %tok.1, bf16[128,1024]{1,0:T(8,128)(2,1)} %cot.1, bf16[8,256,256]{2,1,0:T(8,128)(2,1)} %bitcast.13, bf16[8,256,256]{2,1,0:T(8,128)(2,1)} %bitcast.14, ...), custom_call_target="tpu_custom_call" | custom-call | tf_op jit(solution)/shard_map/pallas_call | solution.py:585
  175.5 4.0 %shard_map.94 = (bf16[128,1024]{1,0:T(8,128)(2,1)}, bf16[128,1024]{1,0:T(8,128)(2,1)}, bf16[8,256,256]{2,1,0:T(8,128)(2,1)}, bf16[8,256,256]{2,1,0:T(8,128)(2,1)}) custom-call(bf16[128,1024]{1,0:T(8,128)(2,1)} %get-tuple-element.12.refs_0_, bf16[128,1024]{1,0:T(8,128)(2,1)} %get-tuple-element.13.refs_1_, bf16[8,256,256]{2,1,0:T(8,128)(2,1)} %get-tuple-element.14.refs_2_, ...), custom_call_target="tpu_custom_call" | custom-call | tf_op jit(solution)/shard_map/pallas_call | solution.py:602
  (5 shorter events, 0.0 us)
Async XLA Ops:
  1.3 0.7 copy-start

commit v5 on v4

--- a/solution.py
+++ b/solution.py
@@ -136,85 +136,71 @@
 
 
 class RowGather:
-    def __init__(self, copies, own, dest, local, early=None):
-        self.copies, self.own, self.dest, self.local, self.early = copies, own, dest, local, early
-        self.overs = []
-        if early is not None:
-            self.early_copy = copies.start(own, early, zh=1)
-
-    def spread(self):
-        self.mine, self.spread_copies = [], []
-        sources = [self.own]
-        if self.early is not None:
-            self.early_copy.wait_recv()
-            sources.append(self.early)
+    def __init__(self, copies, own, dest, local):
+        self.mine, self.spread_copies, make = [], [], copies.make
         for r in (0, 1, 3, 2):
             rows = pl.ds(pl.multiple_of(lax.rem(y_index() + r, 4) * QUARTER, QUARTER), QUARTER)
-            for zh, source in enumerate(sources):
-                for d in range(4):
-                    piece = source.at[rows, block(d)]
-                    place = self.dest.at[(4 - r) % 4, d, span(zh * QUARTER, QUARTER)]
-                    if r == 0:
-                        copy = pltpu.make_async_copy(piece, place, self.local.at[len(self.mine)])
-                        copy.start()
-                        self.mine.append(copy)
-                    else:
-                        self.spread_copies.append(self.copies.start(piece, place, dy=r))
-
-    def wait_spread(self):
+            for d in range(4):
+                piece = own.at[rows, block(d)]
+                place = dest.at[(4 - r) % 4, d, span(0, QUARTER)]
+                if r == 0:
+                    self.mine.append(pltpu.make_async_copy(piece, place, local.at[d]))
+                else:
+                    self.spread_copies.append(make(piece, place, dy=r))
+
+        def both_ways(zh):
+            held = dest.at[part(0, 0, zh)]
+            return make(held, dest.at[part(0, 3, zh)], dx=1), make(held, dest.at[part(0, 1, zh)], dx=3)
+
+        self.across = make(dest.at[part(0, 0, 0)], dest.at[part(0, 0, 1)], zh=1)
+        self.first, self.next = both_ways(0), both_ways(1)
+        self.on_up = make(dest.at[part(0, 3, 0)], dest.at[part(0, 2, 0)], dx=1)
+        self.on_down = make(dest.at[part(0, 1, 1)], dest.at[part(0, 2, 1)], dx=3)
+        self.over = [make(dest.at[part(0, x, 0, 2)], dest.at[part(1, x, 0, 2)], core=1) for x in range(4)]
+        self.all = self.spread_copies + [self.across, *self.first, *self.next, self.on_up, self.on_down] + self.over
+
+    def spread(self):
+        for copy in self.mine + self.spread_copies:
+            copy.start()
+
+    def cross(self):
         for copy in self.mine:
             copy.wait()
         for copy in self.spread_copies:
             copy.wait_recv()
-
-    def both_ways(self, zh):
-        own = self.dest.at[part(0, 0, zh)]
-        return (
-            self.copies.start(own, self.dest.at[part(0, 3, zh)], dx=1),
-            self.copies.start(own, self.dest.at[part(0, 1, zh)], dx=3),
-        )
-
-    def over(self, x):
-        self.overs.append(
-            self.copies.start(self.dest.at[part(0, x, 0, 2)], self.dest.at[part(1, x, 0, 2)], core=1))
+        self.across.start()
 
     def begin(self):
-        self.wait_spread()
-        if self.early is None:
-            self.across = self.copies.start(self.dest.at[part(0, 0, 0)], self.dest.at[part(0, 0, 1)], zh=1)
-            self.first = self.both_ways(0)
-        else:
-            up_0, down_0 = self.both_ways(0)
-            up_1, down_1 = self.both_ways(1)
-            self.first, self.next = (up_0, down_0), (up_1, down_1)
-            self.over(0)
+        for copy in self.first:
+            copy.start()
 
     def onward_up(self):
         self.first[0].wait_recv()
-        self.on_up = self.copies.start(self.dest.at[part(0, 3, 0)], self.dest.at[part(0, 2, 0)], dx=1)
+        self.on_up.start()
 
     def second(self):
         self.across.wait_recv()
-        self.next = self.both_ways(1)
-        self.over(0)
+        for copy in self.next:
+            copy.start()
+        self.over[0].start()
 
     def onward_down(self):
         self.next[1].wait_recv()
-        self.on_down = self.copies.start(self.dest.at[part(0, 1, 1)], self.dest.at[part(0, 2, 1)], dx=3)
+        self.on_down.start()
 
     def over_near(self):
         self.next[0].wait_recv()
-        self.over(3)
+        self.over[3].start()
         self.first[1].wait_recv()
-        self.over(1)
+        self.over[1].start()
 
     def over_far(self):
         self.on_up.wait_recv()
         self.on_down.wait_recv()
-        self.over(2)
+        self.over[2].start()
 
     def finish(self):
-        for copy in self.overs:
+        for copy in self.over:
             copy.wait_recv()
 
 
@@ -238,32 +224,39 @@
 
 class RingReduce:
     def __init__(self, copies, part, far, near, axis):
-        self.copies, self.part, self.far, self.near = copies, part, far, near
-        self.up, self.down = {axis: 1}, {axis: 3}
+        self.part, self.far, self.near = part, far, near
+        up, down, make = {axis: 1}, {axis: 3}, copies.make
+        self.far_up = make(part(2, 0), far.at[0], **up)
+        self.far_down = make(part(2, 1), far.at[1], **down)
+        self.near_up = make(part(1, 1), near.at[0, 1], **up)
+        self.near_down = make(part(3, 0), near.at[1, 0], **down)
+        self.last_up = make(far.at[0], near.at[0, 0], **up)
+        self.last_down = make(far.at[1], near.at[1, 1], **down)
 
     def start_far(self):
-        self.far_up = self.copies.start(self.part(2, 0), self.far.at[0], **self.up)
-        self.far_down = self.copies.start(self.part(2, 1), self.far.at[1], **self.down)
+        self.far_up.start()
+        self.far_down.start()
 
     def start_up(self):
-        self.near_up = self.copies.start(self.part(1, 1), self.near.at[0, 1], **self.up)
+        self.near_up.start()
 
     def start_down(self):
-        self.near_down = self.copies.start(self.part(3, 0), self.near.at[1, 0], **self.down)
+        self.near_down.start()
 
     def onward(self):
         self.far_up.wait_recv()
         add_into(self.far.at[0], self.far.at[0], self.part(1, 0))
-        self.last_up = self.copies.start(self.far.at[0], self.near.at[0, 0], **self.up)
+        self.last_up.start()
         self.far_down.wait_recv()
         add_into(self.far.at[1], self.far.at[1], self.part(3, 1))
-        self.last_down = self.copies.start(self.far.at[1], self.near.at[1, 1], **self.down)
+        self.last_down.start()
 
     def finish(self, dst):
         for h, arrivals in enumerate(((self.near_down, self.last_up), (self.near_up, self.last_down))):
             for copy in arrivals:
                 copy.wait_recv()
-            add_into(dst(h), self.part(0, h), self.near.at[0, h], self.near.at[1, h])
+            for n in range(4):
+                add_into(dst(h, n), self.part(0, h).at[n], self.near.at[0, h, n], self.near.at[1, h, n])
 
 
 def weight_part(partial):
@@ -273,14 +266,14 @@
 class OutputReduce:
     def __init__(self, copies, t, partial, arrived, far, near, mid, home):
         self.copies, self.t, self.partial, self.arrived, self.mid, self.home = copies, t, partial, arrived, mid, home
-        self.ring = RingReduce(copies, lambda r, h: arrived.at[span(r * 64 + h * 32, 32)], far, near, "dx")
+        self.ring = RingReduce(copies, lambda r, h: arrived.at[:, span(r * 64 + h * 32, 32)], far, near, "dx")
 
     def start(self):
-        self.over = self.copies.start(self.partial.at[span(256, 256)], self.arrived, core=1)
+        self.over = self.copies.start(self.partial.at[:, span(256, 256)], self.arrived, core=1)
 
     def join(self, r):
         rows = span(64 * r, 64)
-        add_into(self.arrived.at[rows], self.arrived.at[rows], self.partial.at[rows])
+        add_into(self.arrived.at[:, rows], self.arrived.at[:, rows], self.partial.at[:, rows])
 
     def begin(self):
         self.over.wait_recv()
@@ -293,7 +286,7 @@
         self.join(0)
 
     def finish(self):
-        self.ring.finish(lambda h: self.mid.at[span(32 * h, 32)])
+        self.ring.finish(lambda h, n: self.mid.at[span(32 * h, 32), block(n)])
 
     def across(self):
         self.across_copy = self.copies.start(self.mid.at[span(32, 32)], self.home, zh=1)
@@ -315,10 +308,6 @@
             self.last.wait_recv()
 
 
-def columns(d):
-    return pl.ds(pl.multiple_of(d * BLK, BLK), BLK)
-
-
 def dot(a, b, da, db):
     return lax.dot_general(a, b, (((da,), (db,)), ((), ())), preferred_element_type=f32)
 
@@ -336,11 +325,11 @@
 def model_tile(hidden, weights, tab, t, result, flipped, blocks, add=False):
     def step(n, carry):
         for d in (2 * n, 2 * n + 1):
-            total = result[t, :, columns(d)].astype(f32) if add else None
+            total = result[t, d].astype(f32) if add else None
             for h in blocks:
                 product = dot(hidden[h], weights[t][tab[t, 0, d * HIDDEN_BLOCKS + h]], 1, int(flipped))
                 total = product if total is None else total + product
-            result[t, :, columns(d)] = total.astype(bf16)
+            result[t, d] = total.astype(bf16)
         return carry
 
     lax.fori_loop(0, 2, step, 0)
@@ -371,17 +360,20 @@
                  tok_all, cot_all, w1_0, w1_1, w1_2, w1_3, w2_0, w2_1, w2_2, w2_3,
                  slope_all, hid, hid_other, grad, grad_other, act, model_part, second_part, first_part,
                  far_s, near_s, far_f, near_f, arrived_o, far_o, near_o, mid_o, home_o,
-                 arrived_i, far_i, near_i, mid_i, home_i, cot_early, tab_all, tab, send, recv, local):
+                 arrived_i, far_i, near_i, mid_i, home_i, tab_all, tab, send, recv, local):
     greet(Y_PEERS + X_PEERS + [CORE_PEER, ZH_PEER, ZL_PEER])
     copies = Copies(send, recv)
     core = lax.rem(lax.axis_index("col"), 2)
     first_w, second_w = (w1_0, w1_1, w1_2, w1_3), (w2_0, w2_1, w2_2, w2_3)
+    on_first, on_second = pl.when(core == 0), pl.when(core == 1)
     tokens = RowGather(copies, tok, tok_all, local.at[span(14, 4)])
+    cotangent = RowGather(copies, cot, cot_all, local.at[span(18, 4)])
+    w1_ring = WeightGather(copies, w1, first_w)
+    w2_ring = WeightGather(copies, w2, second_w)
     tokens.spread()
-    w1_ring = WeightGather(copies, w1, first_w)
-    on_first, on_second = pl.when(core == 0), pl.when(core == 1)
+    tabs = [copies.start(tab_in, tab_all.at[4 - r], dy=r) for r in (1, 2, 3)]
+    cotangent.spread()
     on_first(w1_ring.start)
-    tabs = [copies.start(tab_in, tab_all.at[4 - r], dy=r) for r in (1, 2, 3)]
     tab_mine = pltpu.make_async_copy(tab_in, tab_all.at[0], local.at[1])
     tab_mine.start()
     w1_mine = pltpu.make_async_copy(w1, w1_0.at[span(0, SLOTS)], local.at[2])
@@ -390,16 +382,22 @@
     w2_mine.start()
     for weights in first_w + second_w:
         weights[SLOTS] = jnp.zeros((BLK, BLK), bf16)
+    tokens.cross()
     tokens.begin()
+    cotangent.cross()
     tokens.onward_up()
-    on_first(w1_ring.forward)
+
+    @on_first
+    def _():
+        w1_ring.forward()
+        w2_ring.start()
+
     tokens.second()
+    tokens.onward_down()
+    cotangent.begin()
     on_second(w1_ring.start)
-    cotangent = RowGather(copies, cot, cot_all, local.at[span(18, 8)], cot_early)
-    tokens.onward_down()
     tokens.over_near()
     tokens.over_far()
-    on_second(w1_ring.forward)
     for copy in tabs:
         copy.wait_recv()
     tab_mine.wait()
@@ -408,9 +406,22 @@
     tab_down.wait()
     tokens.finish()
     w1_mine.wait()
+
+    def rest_of_cotangent():
+        cotangent.onward_down()
+        cotangent.over_near()
+        cotangent.over_far()
+
+    @on_second
+    def _():
+        cotangent.onward_up()
+        cotangent.second()
+        rest_of_cotangent()
+        w1_ring.forward()
+        w2_ring.start()
+
     for r in (3, 1, 2):
         w1_ring.wait(r)
-    w2_ring = WeightGather(copies, w2, second_w)
 
     swap = copies.reserve(HIDDEN_BLOCKS)
     back = copies.reserve(HIDDEN_BLOCKS)
@@ -427,42 +438,35 @@
         return carry
 
     lax.fori_loop(0, 4, make_hidden, 0)
-    cotangent.spread()
-    w2_ring.start()
-    cotangent.begin()
+
+    @on_first
+    def _():
+        cotangent.onward_up()
+        cotangent.second()
+
+    w2_ring.forward()
     lax.fori_loop(4, 8, make_hidden, 0)
-    cotangent.onward_up()
-    w2_ring.forward()
-    cotangent.onward_down()
+    on_first(rest_of_cotangent)
+
+    def make_grad(h, carry):
+        grad[h] = hidden_block(cot_all, second_w, tab, h, True)
+        back_copy(h).start()
+        return carry
+
+    cotangent.finish()
+    w2_mine.wait()
+    for r in (3, 1, 2):
+        w2_ring.wait(r)
+    lax.fori_loop(0, 8, make_grad, 0)
 
     def activate(h, rows):
         value, slope = gelu_pair(hid[h, rows].astype(f32) + hid_other[h, rows].astype(f32))
         act[h, rows] = value.astype(bf16)
         slope_all[h, rows] = slope
 
-    def activations(*blocks):
-        for h in blocks:
-            swap_copy(h).wait_recv()
-            over_chunks(h, activate)
-
-    activations(0, 1)
-    cotangent.over_near()
-    cotangent.over_far()
-    activations(2, 3)
-    cotangent.finish()
-    w2_mine.wait()
-
-    def make_grad(h, carry):
-        grad[h] = hidden_block(cot_all, second_w, tab, h, True)
-        return carry
-
-    for r in (3, 1, 2):
-        w2_ring.wait(r)
-    lax.fori_loop(0, 4, make_grad, 0)
-    activations(4, 5, 6)
-    for h in range(4):
-        back_copy(h).start()
-    activations(7)
+    for h in range(HIDDEN_BLOCKS):
+        swap_copy(h).wait_recv()
+        over_chunks(h, activate)
 
     seconds = RingReduce(copies, weight_part(second_part), far_s, near_s, "dy")
 
@@ -475,13 +479,7 @@
         ring.start_down()
         slot_grads(tab, 0, hidden, rows, result, hidden_left)
 
-    def make_rest(h, carry):
-        make_grad(h, carry)
-        back_copy(h).start()
-        return carry
-
     begin_ring(seconds, act, cot_all, second_part, True)
-    lax.fori_loop(4, 8, make_rest, 0)
     order = (2, 1, 3, 0)
     every = tuple(range(HIDDEN_BLOCKS))
     outs = {t: OutputReduce(copies, t, model_part.at[t], arrived_o.at[t], far_o.at[t], near_o.at[t], mid_o.at[t], home_o.at[t])
@@ -502,36 +500,51 @@
             back_copy(h).wait_recv()
             over_chunks(h, combine)
 
-    combined(0, 1)
-    for t in order:
-        outs[t].begin()
-    combined(2, 3)
-    for t in order:
-        outs[t].ring.onward()
+
+    def begin_outputs():
+        for t in order:
+            outs[t].begin()
+
+    def onward_outputs():
+        for t in order:
+            outs[t].ring.onward()
+
+    on_second(begin_outputs)
+    combined(0, 1, 2, 3)
+
+    copies.sent(*cotangent.all)
+    for t in order:
+        model_tile(hid, first_w, tab, t, cot_all, True, every[:4])
+    on_second(onward_outputs)
     combined(4, 5)
-
-    copies.sent(*[outs[t].over for t in order])
-    for t in order:
-        model_tile(hid, first_w, tab, t, model_part, True, every[:6])
+    for t in order:
+        model_tile(hid, first_w, tab, t, cot_all, True, every[4:6], True)
     combined(6, 7)
     firsts = RingReduce(copies, weight_part(first_part), far_f, near_f, "dy")
-    ins = {t: OutputReduce(copies, t, model_part.at[t], arrived_i.at[t], far_i.at[t], near_i.at[t], mid_i.at[t], home_i.at[t])
+    ins = {t: OutputReduce(copies, t, cot_all.at[t], arrived_i.at[t], far_i.at[t], near_i.at[t], mid_i.at[t], home_i.at[t])
            for t in order}
+    for t in order:
+        model_tile(hid, first_w, tab, t, cot_all, True, every[6:], True)
+        ins[t].start()
     begin_ring(firsts, hid, tok_all, first_part, False)
-    for t in order:
-        model_tile(hid, first_w, tab, t, model_part, True, every[6:], True)
-        ins[t].start()
-    for t in order:
-        ins[t].begin()
+
+    @on_first
+    def _():
+        firsts.onward()
+        begin_outputs()
+        onward_outputs()
+
     for t in order:
         outs[t].finish()
         outs[t].across()
-    firsts.onward()
+    for t in order:
+        ins[t].begin()
+    on_second(firsts.onward)
     for t in order:
         outs[t].send_home(output, local.at[6])
     for t in order:
         ins[t].ring.onward()
-    seconds.finish(lambda h: second_part.at[0, (LO, HI)[h]])
+    seconds.finish(lambda h, n: second_part.at[0, 4 * h + n])
     second_out = pltpu.make_async_copy(second_part.at[0], second_grad, local.at[7])
     second_out.start()
     for t in order:
@@ -539,7 +552,7 @@
         ins[t].across()
     for t in order:
         ins[t].send_home(input_grad, local.at[8])
-    firsts.finish(lambda h: first_part.at[0, (LO, HI)[h]])
+    firsts.finish(lambda h, n: first_part.at[0, 4 * h + n])
     first_out = pltpu.make_async_copy(first_part.at[0], first_grad, local.at[9])
     first_out.start()
     for t in order:
@@ -560,7 +573,6 @@
 ANY = pl.BlockSpec(memory_space=pl.ANY)
 HIDDEN = (HIDDEN_BLOCKS, ROWS, BLK)
 TILE = (SLOTS, BLK, BLK)
-MODEL = (4, ROWS, WIDTH)
 DMA = pltpu.SemaphoreType.DMA
 
 
@@ -580,7 +592,7 @@
 
 def per_device(tokens, w1_blocks, w2_blocks, block_places, counts, cotangent):
     weight_ring = [vmem(2, 4, BLK, BLK), vmem(2, 2, 4, BLK, BLK)]
-    output_ring = [vmem(4, 256, WIDTH), vmem(4, 2, 32, WIDTH), vmem(4, 2, 2, 32, WIDTH), vmem(4, 64, WIDTH), vmem(4, 32, WIDTH)]
+    output_ring = [vmem(4, 4, 256, BLK), vmem(4, 2, 4, 32, BLK), vmem(4, 2, 2, 4, 32, BLK), vmem(4, 64, WIDTH), vmem(4, 32, WIDTH)]
     shapes = [jax.ShapeDtypeStruct(dims, bf16) for dims in ((128, WIDTH), (128, WIDTH), TILE, TILE)]
     results = pl.pallas_call(
         layer_kernel,
@@ -590,9 +602,8 @@
         scratch_shapes=[vmem(4, 4, ROWS, BLK)] * 2
         + [vmem(SLOTS + 1, BLK, BLK)] * 8
         + [pltpu.VMEM(HIDDEN, f32)] + [vmem(*HIDDEN)] * 5
-        + [vmem(*MODEL)] + [vmem(4, *TILE)] * 2
+        + [vmem(4, 4, ROWS, BLK)] + [vmem(4, *TILE)] * 2
         + weight_ring * 2 + output_ring * 2
-        + [vmem(128, WIDTH)]
         + [pltpu.VMEM((4, 8, 128), jnp.int32), pltpu.SMEM((4, 8, 128), jnp.int32)]
         + [DMA((200,)), DMA((200,)), DMA((26,))],
         compiler_params=pltpu.CompilerParams(

time: 183 us -> 180 us (0.984); the launches traced: 180 us -> 179 us
  no operation moved by 1% of the time
where the time goes in v5:
time: 180 us; the launch traced here: 179 us
  Pallas kernels  177 us (98%)
    pallas_call x1, Pallas kernels, per_device(): pl.pallas_call(layer_kernel, out_shape=shapes, in_specs=[ANY] * 5, out_sp...  173 us
    pallas_call x1, Pallas kernels, per_device(): pl.pallas_call(place_kernel, grid=(4,), out_shape=shapes, in_specs=blocks...  3.99 us

profile of v5, /device:TPU:0, one launch (start us, length us, event | category | flops | bytes accessed | tf_op | source)
XLA Modules:
  0.0 179.4 jit_solution(16896533255419732192)
XLA Ops:
  1.3 0.0 copy-start
  1.3 0.6 copy-done
  1.9 0.1 multiply_reduce_fusion
  2.1 0.1 concatenate.3
  2.1 0.6 broadcast_in_dim.9.tab_in
  2.7 172.6 %shard_map.93 = (bf16[128,1024]{1,0:T(8,128)(2,1)}, bf16[128,1024]{1,0:T(8,128)(2,1)}, bf16[8,256,256]{2,1,0:T(8,128)(2,1)}, bf16[8,256,256]{2,1,0:T(8,128)(2,1)}) custom-call(bf16[128,1024]{1,0:T(8,128)(2,1)} %tok.1, bf16[128,1024]{1,0:T(8,128)(2,1)} %cot.1, bf16[8,256,256]{2,1,0:T(8,128)(2,1)} %bitcast.13, bf16[8,256,256]{2,1,0:T(8,128)(2,1)} %bitcast.14, ...), custom_call_target="tpu_custom_call" | custom-call | tf_op jit(solution)/shard_map/pallas_call | solution.py:597
  175.4 4.0 %shard_map.94 = (bf16[128,1024]{1,0:T(8,128)(2,1)}, bf16[128,1024]{1,0:T(8,128)(2,1)}, bf16[8,256,256]{2,1,0:T(8,128)(2,1)}, bf16[8,256,256]{2,1,0:T(8,128)(2,1)}) custom-call(bf16[128,1024]{1,0:T(8,128)(2,1)} %get-tuple-element.12.refs_0_, bf16[128,1024]{1,0:T(8,128)(2,1)} %get-tuple-element.13.refs_1_, bf16[8,256,256]{2,1,0:T(8,128)(2,1)} %get-tuple-element.14.refs_2_, ...), custom_call_target="tpu_custom_call" | custom-call | tf_op jit(solution)/shard_map/pallas_call | solution.py:613
  (5 shorter events, 0.0 us)
Async XLA Ops:
  1.3 0.7 copy-start

commit v6 on v5

--- a/solution.py
+++ b/solution.py
@@ -384,8 +384,8 @@
         weights[SLOTS] = jnp.zeros((BLK, BLK), bf16)
     tokens.cross()
     tokens.begin()
+    tokens.onward_up()
     cotangent.cross()
-    tokens.onward_up()
 
     @on_first
     def _():
@@ -566,8 +566,16 @@
 
 
 def place_kernel(*refs):
-    for source, dest in zip(refs[:4], refs[4:]):
-        dest[...] = source[...]
+    sources, dests, held, sems = refs[:4], refs[4:8], refs[8:12], refs[12]
+    loads = [pltpu.make_async_copy(a, b, sems.at[n]) for n, (a, b) in enumerate(zip(sources, held))]
+    stores = [pltpu.make_async_copy(a, b, sems.at[4 + n]) for n, (a, b) in enumerate(zip(held, dests))]
+    for copy in loads:
+        copy.start()
+    for load, store in zip(loads, stores):
+        load.wait()
+        store.start()
+    for copy in stores:
+        copy.wait()
 
 
 ANY = pl.BlockSpec(memory_space=pl.ANY)
@@ -609,9 +617,9 @@
         compiler_params=pltpu.CompilerParams(
             collective_id=0, has_side_effects=True, vmem_limit_bytes=62 * MIB),
     )(tokens, cotangent, w1_blocks[0, 0], w2_blocks[0, 0], table(block_places, counts))
-    blocks = [pl.BlockSpec((32, WIDTH), lambda n: (n, 0))] * 2 + [pl.BlockSpec((2, BLK, BLK), lambda n: (n, 0, 0))] * 2
     output, input_grad, first_grad, second_grad = pl.pallas_call(
-        place_kernel, grid=(4,), out_shape=shapes, in_specs=blocks, out_specs=blocks,
+        place_kernel, out_shape=shapes, in_specs=[ANY] * 4, out_specs=[ANY] * 4,
+        scratch_shapes=[vmem(*one.shape) for one in shapes] + [DMA((8,))],
     )(*results)
     return (output, input_grad, first_grad[None, None], second_grad[None, None])
 

time: 180 us -> 178 us (0.989)
  Pallas kernels: 177 us -> 175 us
where the time goes in v6:
time: 178 us
  Pallas kernels  175 us (98%)
    pallas_call x1, Pallas kernels, per_device(): pl.pallas_call(layer_kernel, out_shape=shapes, in_specs=[ANY] * 5, out_sp...  173 us

profile of v6, /device:TPU:0, one launch (start us, length us, event | category | flops | bytes accessed | tf_op | source)
XLA Modules:
  0.0 178.3 jit_solution(618061832904514572)
XLA Ops:
  1.3 0.0 copy-start
  1.3 0.6 copy-done
  1.9 0.1 multiply_reduce_fusion
  2.1 0.1 concatenate.3
  2.1 0.6 broadcast_in_dim.9.tab_in
  2.7 172.6 %shard_map.93 = (bf16[128,1024]{1,0:T(8,128)(2,1)}, bf16[128,1024]{1,0:T(8,128)(2,1)}, bf16[8,256,256]{2,1,0:T(8,128)(2,1)}, bf16[8,256,256]{2,1,0:T(8,128)(2,1)}) custom-call(bf16[128,1024]{1,0:T(8,128)(2,1)} %tok.1, bf16[128,1024]{1,0:T(8,128)(2,1)} %cot.1, bf16[8,256,256]{2,1,0:T(8,128)(2,1)} %bitcast.13, bf16[8,256,256]{2,1,0:T(8,128)(2,1)} %bitcast.14, ...), custom_call_target="tpu_custom_call" | custom-call | tf_op jit(solution)/shard_map/pallas_call | solution.py:605
  175.3 2.8 %shard_map.94 = (bf16[128,1024]{1,0:T(8,128)(2,1)}, bf16[128,1024]{1,0:T(8,128)(2,1)}, bf16[8,256,256]{2,1,0:T(8,128)(2,1)}, bf16[8,256,256]{2,1,0:T(8,128)(2,1)}) custom-call(bf16[128,1024]{1,0:T(8,128)(2,1)} %get-tuple-element.12.refs_0_, bf16[128,1024]{1,0:T(8,128)(2,1)} %get-tuple-element.13.refs_1_, bf16[8,256,256]{2,1,0:T(8,128)(2,1)} %get-tuple-element.14.refs_2_, ...), custom_call_target="tpu_custom_call" | custom-call | tf_op jit(solution)/shard_map/pallas_call | solution.py:620
  (5 shorter events, 0.0 us)
Async XLA Ops:
  1.3 0.7 copy-start
